TPU v7x, 128 devices: a whole 4x4x4 slice. The times are simulated.
128 devices in a mesh: ctx: 32 (over y, x, core), head: 4 (over z).
Axes of the slice: x: 4, y: 4, z: 4, core: 2. Of those that a mesh axis runs over, the one named last changes fastest.
Arguments:
- inputs: bfloat16 [16384, 4096], P('ctx'), may hold values from -8 to 8
- query_weight: bfloat16 [4096, 2048], P(None, 'head'), may hold values from -0.09375 to 0.09375
- key_weight: bfloat16 [4096, 512], P(None, 'head'), may hold values from -0.09375 to 0.09375
- value_weight: bfloat16 [4096, 512], P(None, 'head'), may hold values from -0.09375 to 0.09375
- out_grad: bfloat16 [16384, 2048], P('ctx', 'head'), may hold values from -6 to 6
- doc_lengths: int32 [32], replicated, may hold values from 128 to 1536, as said below
Outputs:
- attn_out: bfloat16 [16384, 2048], P('ctx', 'head')
- input_grad: bfloat16 [16384, 4096], P('ctx', 'head')
- query_weight_grad: float32 [4096, 2048], P('ctx', 'head')
- key_weight_grad: float32 [4096, 512], P('ctx', 'head')
- value_weight_grad: float32 [4096, 512], P('ctx', 'head')
Inputs may be any that keep to these rules, and one draw needn't show every extreme that they name: `doc_lengths`: each length is a positive multiple of 128; the lengths sum to 16384; the largest is exactly 1536.
All inputs are finite; a program needn't handle non-finite values.
Results may differ from a plain program's by a relative error of at most 0.018.
The roundings to bfloat16 on the way count: a program that leaves them out, or rounds other values in their place, can miss the bound.
Values may be sent and summed in bfloat16 or wider, within the bound.
A program may use at most 128 MiB of HBM per device.

v0:
```python
from functools import partial

import jax
import jax.numpy as jnp
from jax import lax
from jax.sharding import PartitionSpec as P

HD = 128
GROUP = 4
KV_DEV = 1
SPAN = 3


NEG = -1e30


def from_behind(value, axis, steps):
    count = lax.axis_size(axis)
    initial, last = (max(0, -steps), min(count, count - steps))
    return lax.ppermute(value, axis, [(source, source + steps) for source in range(initial, last)])


def visible(query_pos, query_start, key_pos):
    return (key_pos[None, :] >= query_start[:, None]) & (key_pos[None, :] <= query_pos[:, None])


def scores_of(query_blk, key_blk, factor):
    return (
        jnp.einsum("qkgd,skd->kgqs", query_blk, key_blk, preferred_element_type=jnp.float32)
        * factor
    )


def keep_carry(carry, *others):
    return carry


def stats_live(carry, query_blk, key_blk, mask, factor):
    run_top, run_total = carry
    score = jnp.where(mask, scores_of(query_blk, key_blk, factor), NEG)
    new_top = jnp.maximum(run_top, jnp.max(score, axis=-1))
    weight = jnp.where(mask, jnp.exp(score - new_top[..., None]), 0.0)
    return (new_top, run_total * jnp.exp(run_top - new_top) + jnp.sum(weight, axis=-1))


def output_live(accum, query_blk, key_blk, value_blk, mask, lse_blk, factor):
    prob = jnp.where(mask, jnp.exp(scores_of(query_blk, key_blk, factor) - lse_blk[..., None]), 0.0)
    return accum + jnp.einsum(
        "kgqs,skd->qkgd", prob.astype(jnp.bfloat16), value_blk, preferred_element_type=jnp.float32
    )


def grads_live(carry, query_blk, key_blk, value_blk, grad_blk, mask, lse_blk, delta_blk, factor):
    query_acc, key_acc, value_acc = carry
    prob = jnp.where(mask, jnp.exp(scores_of(query_blk, key_blk, factor) - lse_blk[..., None]), 0.0)
    prob_low = prob.astype(jnp.bfloat16)
    dprob = jnp.einsum("qkgd,skd->kgqs", grad_blk, value_blk, preferred_element_type=jnp.float32)
    dscore = (prob * (dprob - delta_blk[..., None])).astype(jnp.bfloat16)
    query_acc = query_acc + factor * jnp.einsum(
        "kgqs,skd->qkgd", dscore, key_blk, preferred_element_type=jnp.float32
    )
    key_acc = factor * jnp.einsum(
        "kgqs,qkgd->skd", dscore, query_blk, preferred_element_type=jnp.float32
    )
    value_acc = jnp.einsum("kgqs,qkgd->skd", prob_low, grad_blk, preferred_element_type=jnp.float32)
    return (query_acc, key_acc, value_acc)


def dot_nt(left_mat, right_mat):
    return lax.dot_general(
        left_mat, right_mat, (((1,), (1,)), ((), ())), preferred_element_type=jnp.float32
    )


def body(inputs, query_weight, key_weight, value_weight, out_grad, doc_lengths):
    tok_rows = inputs.shape[0]
    factor = HD ** (-0.5)
    ctx_index = lax.axis_index("ctx")
    q_cols = query_weight.shape[1]
    k_cols = key_weight.shape[1]
    query = jnp.dot(inputs, query_weight, preferred_element_type=jnp.float32).astype(jnp.bfloat16)
    keys_loc = jnp.dot(inputs, key_weight, preferred_element_type=jnp.float32).astype(jnp.bfloat16)
    values_loc = jnp.dot(inputs, value_weight, preferred_element_type=jnp.float32).astype(
        jnp.bfloat16
    )
    query4 = query.reshape(tok_rows, KV_DEV, GROUP, HD)
    keys3 = keys_loc.reshape(tok_rows, KV_DEV, HD)
    values3 = values_loc.reshape(tok_rows, KV_DEV, HD)
    local_pos = jnp.arange(tok_rows, dtype=jnp.int32)
    positions = ctx_index * tok_rows + local_pos
    doc_ends = jnp.cumsum(doc_lengths)
    starts = jnp.sum(
        jnp.where(doc_ends[None, :] <= positions[:, None], doc_lengths[None, :], 0), axis=1
    )
    key_list = [keys3]
    value_list = [values3]
    for distance in range(1, SPAN + 1):
        moved_keys, moved_values = from_behind((keys3, values3), "ctx", distance)
        key_list.append(moved_keys)
        value_list.append(moved_values)
    key_stack = jnp.stack(key_list)
    value_stack = jnp.stack(value_list)
    n_blocks = key_stack.shape[0]
    key_positions = [(ctx_index - blk_idx) * tok_rows + local_pos for blk_idx in range(n_blocks)]
    q_block = min(512, tok_rows)
    stats_fn = partial(stats_live, factor=factor)
    output_fn = partial(output_live, factor=factor)
    grads_fn = partial(grads_live, factor=factor)
    masks = [visible(positions, starts, key_positions[blk_idx]) for blk_idx in range(n_blocks)]
    carry = (
        jnp.full((KV_DEV, GROUP, q_block), NEG, jnp.float32),
        jnp.zeros((KV_DEV, GROUP, q_block), jnp.float32),
    )
    for blk_idx in range(n_blocks):
        carry = lax.cond(
            jnp.any(masks[blk_idx]),
            stats_fn,
            keep_carry,
            carry,
            query4,
            key_stack[blk_idx],
            masks[blk_idx],
        )
    lse_blk = carry[0] + jnp.log(carry[1])
    accum = jnp.zeros((q_block, KV_DEV, GROUP, HD), jnp.float32)
    for blk_idx in range(n_blocks):
        accum = lax.cond(
            jnp.any(masks[blk_idx]),
            output_fn,
            keep_carry,
            accum,
            query4,
            key_stack[blk_idx],
            value_stack[blk_idx],
            masks[blk_idx],
            lse_blk,
        )
    out_parts = accum.astype(jnp.bfloat16)
    attn_out = out_parts.reshape(tok_rows, q_cols)
    grad4 = out_grad.reshape(tok_rows, KV_DEV, GROUP, HD)
    delta_all = jnp.sum(grad4.astype(jnp.float32) * out_parts.astype(jnp.float32), axis=-1)
    key_grads = [jnp.zeros((tok_rows, KV_DEV, HD), jnp.float32) for blk_idx in range(n_blocks)]
    value_grads = [jnp.zeros((tok_rows, KV_DEV, HD), jnp.float32) for blk_idx in range(n_blocks)]
    delta_blk = jnp.transpose(delta_all, (1, 2, 0))
    query_acc = jnp.zeros((q_block, KV_DEV, GROUP, HD), jnp.float32)
    for blk_idx in range(n_blocks):
        mask = masks[blk_idx]
        query_acc, key_grads[blk_idx], value_grads[blk_idx] = lax.cond(
            jnp.any(mask),
            grads_fn,
            keep_carry,
            (query_acc, key_grads[blk_idx], value_grads[blk_idx]),
            query4,
            key_stack[blk_idx],
            value_stack[blk_idx],
            grad4,
            mask,
            lse_blk,
            delta_blk,
        )
    key_total = key_grads[0]
    value_total = value_grads[0]
    for distance in range(1, SPAN + 1):
        back_keys, back_values = from_behind(
            (key_grads[distance], value_grads[distance]), "ctx", -distance
        )
        key_total = key_total + back_keys
        value_total = value_total + back_values
    dq_low = query_acc.reshape(tok_rows, q_cols).astype(jnp.bfloat16)
    dk_low = key_total.reshape(tok_rows, k_cols).astype(jnp.bfloat16)
    dv_low = value_total.reshape(tok_rows, k_cols).astype(jnp.bfloat16)
    partial_grad = (
        dot_nt(dq_low, query_weight) + dot_nt(dk_low, key_weight) + dot_nt(dv_low, value_weight)
    )
    input_grad = lax.psum_scatter(
        partial_grad.astype(jnp.bfloat16), "head", scatter_dimension=1, tiled=True
    )
    joined = jnp.concatenate([dq_low, dk_low, dv_low], axis=1)
    full_term = lax.dot_general(
        inputs, joined, (((0,), (0,)), ((), ())), preferred_element_type=jnp.float32
    )
    own_rows = lax.psum_scatter(full_term, "ctx", scatter_dimension=0, tiled=True)
    return (
        attn_out,
        input_grad,
        own_rows[:, :q_cols],
        own_rows[:, q_cols : q_cols + k_cols],
        own_rows[:, q_cols + k_cols :],
    )


def solution(mesh):
    return jax.shard_map(
        body,
        mesh=mesh,
        in_specs=(
            P("ctx", None),
            P(None, "head"),
            P(None, "head"),
            P(None, "head"),
            P("ctx", "head"),
            P(),
        ),
        out_specs=(
            P("ctx", "head"),
            P("ctx", "head"),
            P("ctx", "head"),
            P("ctx", "head"),
            P("ctx", "head"),
        ),
        check_vma=False,
    )
```

profile of v0, /device:TPU:0, one launch (start us, length us, event | category | flops | bytes accessed | tf_op | source)
XLA Modules:
  0.0 308.8 jit_solution(6708992525551877810)
XLA Ops:
  7.2 1.1 copy-done
  8.4 3.6 %fusion.259 = bf16[512,1,128]{2,0,1:T(8,128)(2,1)S(1)} fusion(bf16[512,4096]{1,0:T(8,128)(2,1)} %param.30, bf16[4096,128]{1,0:T(8,128)(2,1)S(1)} %copy-done), kind=kOutput, calls=%fused_computation.212 | convolution fusion | flops 536936448 | bytes 5373952 | tf_op jit(solution)/shard_map/dot_general | solution.py:82
  12.0 2.0 collective-permute-start
  14.0 4.1 %collective-permute-start.1 = (bf16[512,1,128]{2,0,1:T(8,128)(2,1)S(1)}, bf16[512,1,128]{2,0,1:T(8,128)(2,1)}, u32[]{:S(2)}, u32[]{:S(2)}) collective-permute-start(bf16[512,1,128]{2,0,1:T(8,128)(2,1)S(1)} %fusion.259), channel_id=1, source_target_pairs={{0,8},{4,12},{8,16},{12,20},{16,24},{20,28},{24,32},{28,36},{32,40... | collective-permute-start | bytes 393224 | tf_op jit(solution)/shard_map/ppermute | solution.py:20
  18.1 3.4 %collective-permute-start.2 = (bf16[512,1,128]{2,0,1:T(8,128)(2,1)S(1)}, bf16[512,1,128]{2,0,1:T(8,128)(2,1)S(1)}, u32[]{:S(2)}, u32[]{:S(2)}) collective-permute-start(bf16[512,1,128]{2,0,1:T(8,128)(2,1)S(1)} %fusion.259), channel_id=1, source_target_pairs={{0,12},{4,16},{8,20},{12,24},{16,28},{20,32},{24,36},{28,40},{32,4... | collective-permute-start | bytes 393224 | tf_op jit(solution)/shard_map/ppermute | solution.py:20
  21.5 1.9 fusion.260
  23.4 3.3 %collective-permute-start.3 = (bf16[512,1,128]{2,0,1:T(8,128)(2,1)}, bf16[512,1,128]{2,0,1:T(8,128)(2,1)}, u32[]{:S(2)}, u32[]{:S(2)}) collective-permute-start(bf16[512,1,128]{2,0,1:T(8,128)(2,1)} %fusion.260), channel_id=1, source_target_pairs={{0,4},{4,8},{8,12},{12,16},{16,20},{20,24},{24,28},{28,32},{32,36}... | collective-permute-start | bytes 393224 | tf_op jit(solution)/shard_map/ppermute | solution.py:20
  26.7 2.8 collective-permute-start.4
  29.8 5.9 %convolution_convert_fusion = bf16[512,512]{0,1:T(8,128)(2,1)S(1)} fusion(bf16[512,4096]{1,0:T(8,128)(2,1)} %param.30, bf16[4096,512]{1,0:T(8,128)(2,1)} %param.31), kind=kOutput, calls=%fused_computation.209 | convolution fusion | flops 2147745792 | bytes 8912896 | tf_op jit(solution)/shard_map/dot_general | solution.py:81
  35.8 1.8 fusion.269
  40.2 1.0 copy.102
  41.2 1.9 conditional.17
  41.2 0.9 fusion
  42.1 1.0 select_reduce_fusion
  43.2 4.2 %collective-permute-start.5 = (bf16[512,1,128]{2,0,1:T(8,128)(2,1)}, bf16[512,1,128]{2,0,1:T(8,128)(2,1)}, u32[]{:S(2)}, u32[]{:S(2)}) collective-permute-start(bf16[512,1,128]{2,0,1:T(8,128)(2,1)} %fusion.260), channel_id=1, source_target_pairs={{0,12},{4,16},{8,20},{12,24},{16,28},{20,32},{24,36},{28,40},{32,4... | collective-permute-start | bytes 393224 | tf_op jit(solution)/shard_map/ppermute | solution.py:20
  47.6 3.3 %conditional.21 = (f32[512,1,4,128]{3,0,2,1:T(8,128)S(1)}) conditional(s32[]{:T(128)} %convert_element_type.119, () %tuple.107, (pred[512,512]{0,1:T(8,128)(4,1)S(1)}, bf16[512,1,128]{2,0,1:T(8,128)(2,1)S(1)}, bf16[512,1,4,128]{0,3,2,1:T(8,128)(2,1)S(1)}, f32[1,4,512]{2,1,0:T(4,128)S(1)}, bf16[512,1,128]{2,0,1:T(8,128)(2,1)}) %tuple.227), branch_computations={%region_22.23_spmd, %region_23.24_spmd} | conditional | flops 541065216 | bytes 3678272 | solution.py:127
  47.7 0.7 copy-done.3
  48.4 2.6 fusion.22
  51.1 2.3 conditional.24
  51.1 1.0 copy.134
  52.1 1.3 copy.132
  53.4 1.5 multiply_reduce_fusion
  54.9 13.1 %conditional.25 = (f32[512,1,4,128]{3,0,2,1:T(8,128)S(1)}, f32[512,1,128]{0,2,1:T(8,128)}, f32[512,1,128]{0,2,1:T(8,128)}) conditional(s32[]{:T(128)} %convert_element_type.119, () %tuple.117, (pred[512,512]{0,1:T(8,128)(4,1)}, bf16[512,1,128]{2,0,1:T(8,128)(2,1)}, bf16[512,1,4,128]{0,3,2,1:T(8,128)(2,1)S(1)}, f32[1,4,512]{2,1,0:T(4,128)S(1)}, ...), branch_computations={%region_31.32_spmd, %region_32.33_spmd} | conditional | flops 1352990720 | bytes 44458120 | solution.py:148
  55.4 1.7 fusion.120
  57.1 2.7 fusion.87
  59.8 0.7 fusion.102
  60.6 1.5 fusion.114
  62.0 1.8 copy.136
  63.8 4.2 %fusion.105 = f32[512,1,128]{0,2,1:T(8,128)} fusion(f32[512,512,4]{1,0,2:T(8,128)} %copy-done.1, f32[4,512]{1,0:T(4,128)S(1)} %bitcast.755, pred[512,512]{0,1:T(8,128)(4,1)} %get-tuple-element.229, bf16[512,1,4,128]{0,3,2,1:T(8,128)(2,1)} %get-tuple-element.512), kind=kOutput, calls=%fused_computation.100 | convolution fusion | flops 272629760 | bytes 5251072 | tf_op jit(solution)/shard_map/cond/branch_1_fun/kgqs,qkgd->skd/dot_general | solution.py:65
  68.0 0.7 copy-done.12
  68.8 0.2 conditional.27
  69.1 0.7 copy-done.14
  69.8 1.5 conditional.28
  69.8 0.7 broadcast.242
  70.6 0.7 broadcast.242.clone
  71.3 1.1 copy.119
  72.4 1.3 collective-permute-start.11
  73.7 1.1 copy.118
  74.8 1.3 collective-permute-start.10
  76.1 1.1 copy.116
  77.2 1.3 collective-permute-start.9
  78.5 1.1 copy.115
  79.5 1.3 collective-permute-start.8
  80.8 1.8 copy.114
  82.6 1.3 collective-permute-start.7
  83.9 1.8 copy.112
  85.7 1.3 collective-permute-start.6
  87.2 8.2 %collective-permute-done.10 = f32[512,1,128]{0,2,1:T(8,128)} collective-permute-done((f32[512,1,128]{0,2,1:T(8,128)S(1)}, f32[512,1,128]{0,2,1:T(8,128)}, u32[]{:S(2)}, u32[]{:S(2)}) %collective-permute-start.10) | collective-permute-done | bytes 262176 | tf_op jit(solution)/shard_map/ppermute | solution.py:20
  95.4 1.3 fusion.267
  96.7 4.6 %collective-permute-done.8 = f32[512,1,128]{0,2,1:T(8,128)} collective-permute-done((f32[512,1,128]{0,2,1:T(8,128)S(1)}, f32[512,1,128]{0,2,1:T(8,128)}, u32[]{:S(2)}, u32[]{:S(2)}) %collective-permute-start.8) | collective-permute-done | bytes 262176 | tf_op jit(solution)/shard_map/ppermute | solution.py:20
  101.3 5.9 %collective-permute-done.7 = f32[512,1,128]{0,2,1:T(8,128)} collective-permute-done((f32[512,1,128]{0,2,1:T(8,128)}, f32[512,1,128]{0,2,1:T(8,128)}, u32[]{:S(2)}, u32[]{:S(2)}) %collective-permute-start.7) | collective-permute-done | bytes 262176 | tf_op jit(solution)/shard_map/ppermute | solution.py:20
  107.2 1.3 fusion.266
  108.5 9.2 %convolution_bitcast_fusion = f32[4096,768]{0,1:T(8,128)} fusion(bf16[512,4096]{1,0:T(8,128)(2,1)} %param.30, bf16[512,128]{0,1:T(8,128)(2,1)S(1)} %fusion.267, bf16[512,128]{0,1:T(8,128)(2,1)S(1)} %fusion.266, bf16[512,512]{0,1:T(8,128)(2,1)S(1)} %bitcast.732), kind=kOutput, calls=%fused_computation.208 | convolution fusion | flops 3223584768 | bytes 17563648 | tf_op jit(solution)/shard_map/dot_general | solution.py:179
  117.7 0.3 reduce-scatter.3.cloned.1.call-start
  118.0 4.6 %fusion.275 = f32[512,4096]{1,0:T(8,128)S(1)} fusion(bf16[512,512]{0,1:T(8,128)(2,1)S(1)} %bitcast.733, bf16[4096,512]{1,0:T(8,128)(2,1)} %param.31), kind=kOutput, calls=%fused_computation.240 | convolution fusion | flops 2147483648 | bytes 13107200 | tf_op jit(solution)/shard_map/dot_general | solution.py:70
  122.6 1.3 fusion.276
  123.9 3.3 %add_convert_fusion = bf16[512,4096]{1,0:T(8,128)(2,1)} fusion(f32[512,4096]{1,0:T(8,128)S(1)} %fusion.275, f32[512,4096]{1,0:T(8,128)S(1)} %fusion.276, bf16[512,128]{0,1:T(8,128)(2,1)S(1)} %fusion.267, bf16[4096,128]{1,0:T(8,128)(2,1)S(1)} %copy-done.17), kind=kOutput, calls=%fused_computation.207 | convolution fusion | flops 543162368 | bytes 22151168 | tf_op jit(solution)/shard_map/dot_general | solution.py:70
  127.2 125.0 %reduce-scatter.5.cloned.1.call-done = f32[128,768]{0,1:T(8,128)} async-done(((f32[4096,768]{0,1:T(8,128)}), f32[128,768]{0,1:T(8,128)}) %reduce-scatter.5.cloned.1.call-update) | async-done | bytes 393232 | tf_op jit(solution)/shard_map/reduce_scatter | solution.py:182
  252.2 1.0 slice.12
  253.2 0.8 copy.121
  254.0 0.9 fusion.274
  254.9 0.7 copy.122
  255.6 0.7 copy.123
  256.4 45.4 %reduce-scatter.3.cloned.1.call-done = bf16[512,1024]{1,0:T(8,128)(2,1)} async-done(((bf16[512,4096]{1,0:T(8,128)(2,1)}), bf16[512,1024]{1,0:T(8,128)(2,1)}) %reduce-scatter.3.cloned.1.call-update) | async-done | bytes 1048592 | tf_op jit(solution)/shard_map/reduce_scatter | solution.py:175
  (68 shorter events, 1.3 us)
Async XLA Ops:
  7.2 1.2 copy-start
  7.2 14.3 %copy-start.16 = (bf16[4096,128]{1,0:T(8,128)(2,1)S(1)}, bf16[4096,128]{1,0:T(8,128)(2,1)}, u32[]{:S(2)}) copy-start(bf16[4096,128]{1,0:T(8,128)(2,1)} %param.33) | copy-start | bytes 3145732
  7.2 22.3 %copy-start.21 = (s32[32]{0:T(128)S(1)}, s32[32]{0:T(128)}, u32[]{:S(2)}) copy-start(s32[32]{0:T(128)} %param.35) | copy-start | bytes 388
  7.2 245.0 %reduce-scatter.5.cloned.1.call-start = ((), (), s32[]{:S(2)}) async-start(), calls=%async_computation.3 | async-start | bytes 12976128 | tf_op jit(solution)/shard_map/reduce_scatter | solution.py:182
  8.4 13.1 %copy-start.22 = (bf16[512,4096]{1,0:T(8,128)(2,1)S(1)}, bf16[512,4096]{1,0:T(8,128)(2,1)}, u32[]{:S(2)}) copy-start(bf16[512,4096]{1,0:T(8,128)(2,1)} %param.30) | copy-start | bytes 12582916
  12.0 35.6 %copy-start.9 = (bf16[512,1,128]{2,0,1:T(8,128)(2,1)}, bf16[512,1,128]{2,0,1:T(8,128)(2,1)S(1)}, u32[]{:S(2)}) copy-start(bf16[512,1,128]{2,0,1:T(8,128)(2,1)S(1)} %fusion.259) | copy-start | bytes 393220
  12.0 31.1 %collective-permute-start = (bf16[512,1,128]{2,0,1:T(8,128)(2,1)S(1)}, bf16[512,1,128]{2,0,1:T(8,128)(2,1)}, u32[]{:S(2)}, u32[]{:S(2)}) collective-permute-start(bf16[512,1,128]{2,0,1:T(8,128)(2,1)S(1)} %fusion.259), channel_id=1, source_target_pairs={{0,4},{4,8},{8,12},{12,16},{16,20},{20,24},{24,28},{28,32},{32,36}... | collective-permute-start | bytes 393224 | tf_op jit(solution)/shard_map/ppermute | solution.py:20
  14.0 33.4 %collective-permute-start.1 = (bf16[512,1,128]{2,0,1:T(8,128)(2,1)S(1)}, bf16[512,1,128]{2,0,1:T(8,128)(2,1)}, u32[]{:S(2)}, u32[]{:S(2)}) collective-permute-start(bf16[512,1,128]{2,0,1:T(8,128)(2,1)S(1)} %fusion.259), channel_id=1, source_target_pairs={{0,8},{4,12},{8,16},{12,20},{16,24},{20,28},{24,32},{28,36},{32,40... | collective-permute-start | bytes 393224 | tf_op jit(solution)/shard_map/ppermute | solution.py:20
  18.1 29.5 %collective-permute-start.2 = (bf16[512,1,128]{2,0,1:T(8,128)(2,1)S(1)}, bf16[512,1,128]{2,0,1:T(8,128)(2,1)S(1)}, u32[]{:S(2)}, u32[]{:S(2)}) collective-permute-start(bf16[512,1,128]{2,0,1:T(8,128)(2,1)S(1)} %fusion.259), channel_id=1, source_target_pairs={{0,12},{4,16},{8,20},{12,24},{16,28},{20,32},{24,36},{28,40},{32,4... | collective-permute-start | bytes 393224 | tf_op jit(solution)/shard_map/ppermute | solution.py:20
  23.4 27.6 %collective-permute-start.3 = (bf16[512,1,128]{2,0,1:T(8,128)(2,1)}, bf16[512,1,128]{2,0,1:T(8,128)(2,1)}, u32[]{:S(2)}, u32[]{:S(2)}) collective-permute-start(bf16[512,1,128]{2,0,1:T(8,128)(2,1)} %fusion.260), channel_id=1, source_target_pairs={{0,4},{4,8},{8,12},{12,16},{16,20},{20,24},{24,28},{28,32},{32,36}... | collective-permute-start | bytes 393224 | tf_op jit(solution)/shard_map/ppermute | solution.py:20
  26.7 24.3 %collective-permute-start.4 = (bf16[512,1,128]{2,0,1:T(8,128)(2,1)}, bf16[512,1,128]{2,0,1:T(8,128)(2,1)}, u32[]{:S(2)}, u32[]{:S(2)}) collective-permute-start(bf16[512,1,128]{2,0,1:T(8,128)(2,1)} %fusion.260), channel_id=1, source_target_pairs={{0,8},{4,12},{8,16},{12,20},{16,24},{20,28},{24,32},{28,36},{32,40... | collective-permute-start | bytes 393224 | tf_op jit(solution)/shard_map/ppermute | solution.py:20
  29.8 10.4 %copy-start.18 = (bf16[512,512]{1,0:T(8,128)(2,1)S(1)}, bf16[512,512]{1,0:T(8,128)(2,1)}, u32[]{:S(2)}) copy-start(bf16[512,512]{1,0:T(8,128)(2,1)} %param.34) | copy-start | bytes 1572868
  37.6 10.1 %copy-start.2 = (pred[512,512]{0,1:T(8,128)(4,1)}, pred[512,512]{0,1:T(8,128)(4,1)S(1)}, u32[]{:S(2)}) copy-start(pred[512,512]{0,1:T(8,128)(4,1)S(1)} %get-tuple-element.568) | copy-start | bytes 786436
  43.2 7.9 %collective-permute-start.5 = (bf16[512,1,128]{2,0,1:T(8,128)(2,1)}, bf16[512,1,128]{2,0,1:T(8,128)(2,1)}, u32[]{:S(2)}, u32[]{:S(2)}) collective-permute-start(bf16[512,1,128]{2,0,1:T(8,128)(2,1)} %fusion.260), channel_id=1, source_target_pairs={{0,12},{4,16},{8,20},{12,24},{16,28},{20,32},{24,36},{28,40},{32,4... | collective-permute-start | bytes 393224 | tf_op jit(solution)/shard_map/ppermute | solution.py:20
  47.7 0.7 copy-start.3
  47.7 0.7 copy-start.10
  53.3 1.6 copy-start.19
  55.3 1.7 copy-start.4
  55.3 1.7 copy-start.5
  57.0 3.5 %copy-start.1 = (f32[512,512,4]{1,0,2:T(8,128)}, f32[512,512,4]{1,0,2:T(8,128)S(1)}, u32[]{:S(2)}) copy-start(f32[512,512,4]{1,0,2:T(8,128)S(1)} %fusion.120) | copy-start | bytes 12582916 | tf_op jit(solution)/shard_map/cond
  57.0 2.8 copy-start.11
  68.0 0.7 copy-start.12
  68.0 0.8 copy-start.13
  69.1 0.7 copy-start.14
  69.1 0.8 copy-start.15
  72.4 13.3 %collective-permute-start.11 = (f32[512,1,128]{0,2,1:T(8,128)S(1)}, f32[512,1,128]{0,2,1:T(8,128)S(1)}, u32[]{:S(2)}, u32[]{:S(2)}) collective-permute-start(f32[512,1,128]{0,2,1:T(8,128)S(1)} %copy.119), channel_id=1, source_target_pairs={{12,0},{16,4},{20,8},{24,12},{28,16},{32,20},{36,24},{40,28},{44,3... | collective-permute-start | bytes 786440 | tf_op jit(solution)/shard_map/ppermute | solution.py:20
  74.8 20.7 %collective-permute-start.10 = (f32[512,1,128]{0,2,1:T(8,128)S(1)}, f32[512,1,128]{0,2,1:T(8,128)}, u32[]{:S(2)}, u32[]{:S(2)}) collective-permute-start(f32[512,1,128]{0,2,1:T(8,128)S(1)} %copy.118), channel_id=1, source_target_pairs={{8,0},{12,4},{16,8},{20,12},{24,16},{28,20},{32,24},{36,28},{40,32... | collective-permute-start | bytes 786440 | tf_op jit(solution)/shard_map/ppermute | solution.py:20
  77.2 18.3 %collective-permute-start.9 = (f32[512,1,128]{0,2,1:T(8,128)S(1)}, f32[512,1,128]{0,2,1:T(8,128)}, u32[]{:S(2)}, u32[]{:S(2)}) collective-permute-start(f32[512,1,128]{0,2,1:T(8,128)S(1)} %copy.116), channel_id=1, source_target_pairs={{4,0},{8,4},{12,8},{16,12},{20,16},{24,20},{28,24},{32,28},{36,32}... | collective-permute-start | bytes 786440 | tf_op jit(solution)/shard_map/ppermute | solution.py:20
  79.5 21.7 %collective-permute-start.8 = (f32[512,1,128]{0,2,1:T(8,128)S(1)}, f32[512,1,128]{0,2,1:T(8,128)}, u32[]{:S(2)}, u32[]{:S(2)}) collective-permute-start(f32[512,1,128]{0,2,1:T(8,128)S(1)} %copy.115), channel_id=1, source_target_pairs={{12,0},{16,4},{20,8},{24,12},{28,16},{32,20},{36,24},{40,28},{44,3... | collective-permute-start | bytes 786440 | tf_op jit(solution)/shard_map/ppermute | solution.py:20
  82.6 24.6 %collective-permute-start.7 = (f32[512,1,128]{0,2,1:T(8,128)}, f32[512,1,128]{0,2,1:T(8,128)}, u32[]{:S(2)}, u32[]{:S(2)}) collective-permute-start(f32[512,1,128]{0,2,1:T(8,128)} %copy.114), channel_id=1, source_target_pairs={{8,0},{12,4},{16,8},{20,12},{24,16},{28,20},{32,24},{36,28},{40,32... | collective-permute-start | bytes 786440 | tf_op jit(solution)/shard_map/ppermute | solution.py:20
  85.7 1.3 copy-start.20
  85.7 21.5 %collective-permute-start.6 = (f32[512,1,128]{0,2,1:T(8,128)}, f32[512,1,128]{0,2,1:T(8,128)}, u32[]{:S(2)}, u32[]{:S(2)}) collective-permute-start(f32[512,1,128]{0,2,1:T(8,128)} %copy.112), channel_id=1, source_target_pairs={{4,0},{8,4},{12,8},{16,12},{20,16},{24,20},{28,24},{32,28},{36,32}... | collective-permute-start | bytes 786440 | tf_op jit(solution)/shard_map/ppermute | solution.py:20
  117.7 184.1 %reduce-scatter.3.cloned.1.call-start = ((), (), s32[]{:S(2)}) async-start(), calls=%async_computation.2 | async-start | bytes 5242880 | tf_op jit(solution)/shard_map/reduce_scatter | solution.py:175
  122.5 1.3 copy-start.17
Sparse Core Ops, SparseCore 0:
  117.8 134.3 reduce-scatter.4
  255.3 46.3 reduce-scatter.2
where the time goes:
time: 315 us; the launch traced here: 309 us
  waiting for transfers between devices  189 us (60%)
  matrix products  43.9 us (14%)
  starting transfers between devices  27.8 us (9%)
  local copies, waits for them, and re-layouts  22.4 us (7%)
  between operations  17.3 us (5%)
  other arithmetic  7.23 us (2%)
    reduce_scatter x1, waiting for transfers between devices, body(): lax.psum_scatter(full_term, 'ctx', scatter_dimension=0, tiled=True)  125 us
    reduce_scatter x1, waiting for transfers between devices, body(): lax.psum_scatter(partial_grad.astype(jnp.bfloat16), 'head', scatter_dimen...  45.4 us
    ppermute x12, starting transfers between devices, from_behind(): lax.ppermute(value, axis, [(source, source + steps) for source in range(i...  27.5 us
    ppermute x12, waiting for transfers between devices, from_behind(): lax.ppermute(value, axis, [(source, source + steps) for source in range(i...  18.8 us
    cond x8, local copies, waits for them, and re-layouts, body(): lax.cond(jnp.any(mask), grads_fn, keep_carry, (query_acc, key_grads[blk_i...  9.87 us
    dot_general x1, matrix products, body(): lax.dot_general(inputs, joined, (((0,), (0,)), ((), ())), preferred_eleme...  9.18 us
    dot_general x3, matrix products, dot_nt(): lax.dot_general(left_mat, right_mat, (((1,), (1,)), ((), ())), preferred_...  9.15 us
  transfers between devices with their start and end apart: 14, of which 5 were waited for; matrix products, arithmetic and copies ran while one was open for 12% of the time, Pallas kernels for 0%

commit v1 on v0

v1 whole, which is shorter than its diff:
```python
import functools
import math

import jax
import jax.numpy as jnp
from jax import lax
from jax.experimental import pallas as pl
from jax.experimental.pallas import tpu as pltpu
from jax.sharding import PartitionSpec as P

HD = 128
GROUP = 4
TOK = 512
D = 4096
QB = 256
WIN = 1664
COLS = 768
NEG = -1e30
MESH = pl.DeviceIdType.MESH
F32 = jnp.float32
BF16 = jnp.bfloat16

NN = (((1,), (0,)), ((), ()))
NT = (((1,), (1,)), ((), ()))


def dot(a, b, dims=NN):
    return lax.dot_general(a, b, dims, preferred_element_type=F32)


class Copies:
    def __init__(self, send_sem, recv_sem):
        self.send_sem, self.recv_sem, self.used = send_sem, recv_sem, 0
        self.sent = []

    def make(self, src, dst, device):
        idx = self.used
        self.used += 1
        return pltpu.make_async_remote_copy(
            src_ref=src,
            dst_ref=dst,
            send_sem=self.send_sem.at[idx],
            recv_sem=self.recv_sem.at[idx],
            device_id=device,
            device_id_type=MESH,
        )

    def start(self, src, dst, device):
        copy = self.make(src, dst, device)
        copy.start()
        self.sent.append(copy)
        return copy


N_COPIES = 80


def kernel(
    doc_ref, x_hbm, wq_hbm, wk_hbm, wv_hbm, do_hbm,
    out_ref, ig_ref, wqg_ref, wkg_ref, wvg_ref,
    x_v, w_v, do_v, kv, kT, vT, q_h, doT, acc, bias, xT, xTs, wz, joined, joined_s, jz,
    dkv_send, dkv_sib, dkv_x, r2p, r2m, r1p, r1m, s2, sp, sm, t_f, u2p, u2m, u1p, u1m, t2, tp, tm,
    ig_acc, send_sem, recv_sem, load_sem,
):
    ctx = lax.axis_index("ctx")
    z = lax.axis_index("head")
    chip = ctx // 2
    k = ctx % 2
    y, x = chip // 4, chip % 4
    factor = HD ** -0.5

    def at(yy, xx, kk, zz):
        return ((yy % 4) * 8 + (xx % 4) * 2 + kk, zz % 4)

    def chip_at(pp, kk):
        return ((pp % 16) * 2 + kk, z)

    sib = at(y, x, 1 - k, z)
    z_peer = [None] + [at(y, x, k, z + r) for r in (1, 2, 3)]
    y_peer = [None] + [at(y + r, x, k, z) for r in (1, 2, 3)]
    x_peer = [None] + [at(y, x + r, k, z) for r in (1, 2, 3)]
    nxt, prv = chip_at(chip + 1, k), chip_at(chip + 15, k)
    third = chip_at(jnp.where(k == 1, chip + 2, chip + 14), 1 - k)

    loads = [
        pltpu.make_async_copy(wk_hbm, w_v.at[:, 512:640], load_sem.at[0]),
        pltpu.make_async_copy(wv_hbm, w_v.at[:, 640:768], load_sem.at[1]),
        pltpu.make_async_copy(x_hbm, x_v, load_sem.at[2]),
        pltpu.make_async_copy(wq_hbm, w_v.at[:, 0:512], load_sem.at[3]),
        pltpu.make_async_copy(do_hbm, do_v, load_sem.at[4]),
    ]
    for load in loads:
        load.start()

    barrier = pltpu.get_barrier_semaphore()
    partners = [sib, *z_peer[1:], *y_peer[1:], x_peer[1], x_peer[3], nxt, prv, third]
    for partner in partners:
        pl.semaphore_signal(barrier, inc=1, device_id=partner, device_id_type=MESH)

    copies = Copies(send_sem, recv_sem)

    loads[0].wait()
    loads[1].wait()
    loads[2].wait()
    kv[1536:2048, :] = dot(x_v[...], w_v[:, 512:768]).astype(BF16)
    pl.semaphore_wait(barrier, len(partners))

    own_kv = kv.at[1536:2048]
    kv1 = copies.start(own_kv, kv.at[512:1024], nxt)
    kv2 = copies.make(own_kv, kv.at[1024:1536], sib)
    kv0 = copies.make(own_kv, kv.at[0:512], third)

    @pl.when(k == 0)
    def _():
        kv2.start()

    @pl.when(k == 1)
    def _():
        kv0.start()

    loads[3].wait()
    wz_got = []
    for r in (1, 2, 3):
        rows = pl.multiple_of(((z + r) % 4) * 1024 + y * 256 + k * 128, 128)
        wz_got.append(copies.start(w_v.at[pl.ds(rows, 128), :], wz.at[r - 1, y, k], z_peer[r]))
    for h in range(GROUP):
        if h % 2 == 0:
            both = dot(x_v[...], w_v[:, h * HD : (h + 2) * HD]).astype(BF16)
            q_h[h] = both[:, :HD]
            q_h[h + 1] = both[:, HD:]

    def transpose_x(i, carry):
        own = pl.multiple_of((2 * i + k) * 128, 128)
        other = pl.multiple_of((2 * i + 1 - k) * 128, 128)
        xT[0, i // 4, i % 4] = x_v[:, pl.ds(own, 128)].T
        xT[1, i // 4, i % 4] = x_v[:, pl.ds(other, 128)].T
        return carry

    lax.fori_loop(0, 16, transpose_x, 0)
    x_got = copies.start(xT.at[1], xTs, sib)

    loads[4].wait()
    for h in range(GROUP):
        doT[h] = do_v[:, h * HD : (h + 1) * HD].T

    pos = ctx * TOK + lax.broadcasted_iota(jnp.int32, (1, TOK), 1)
    start = jnp.zeros((1, TOK), jnp.int32)
    end = jnp.int32(0)
    for j in range(32):
        length = doc_ref[j]
        end = end + length
        start = start + jnp.where(pos >= end, length, 0)
    first = start - (ctx - 3) * TOK
    for b in range(2):
        key_pos = 128 + QB * b + lax.broadcasted_iota(jnp.int32, (WIN, QB), 0)
        query_pos = 1536 + QB * b + lax.broadcasted_iota(jnp.int32, (WIN, QB), 1)
        seen = (key_pos >= first[:, b * QB : (b + 1) * QB]) & (key_pos <= query_pos)
        bias[b] = jnp.where(seen, 0.0, NEG)

    wy_got = []
    for got in wz_got:
        got.wait_recv()
    mine = wz.at[:, y, k]
    for r in (1, 2, 3):
        wy_got.append(copies.start(mine, mine, y_peer[r]))

    kv1.wait_recv()
    fwd2 = copies.make(kv.at[512:1024], kv.at[1024:1536], sib)
    fwd0 = copies.make(kv.at[512:1024], kv.at[0:512], sib)

    @pl.when(k == 0)
    def _():
        fwd0.start()
        fwd2.wait_recv()
        kv0.wait_recv()

    @pl.when(k == 1)
    def _():
        fwd2.start()
        kv2.wait_recv()
        fwd0.wait_recv()

    for i in range(4):
        rows = slice(i * 512, (i + 1) * 512)
        kT[:, rows] = kv[rows, 0:HD].T
        vT[:, rows] = kv[rows, HD:].T
    acc[...] = jnp.zeros_like(acc)

    coef = factor * math.log2(math.e)

    def attend(h, b):
        win = pl.ds(pl.multiple_of(128 + QB * b, 128), WIN)
        rows = pl.ds(pl.multiple_of(QB * b, QB), QB)
        cols = pl.ds(h * HD, HD)
        key, value = kv[win, 0:HD], kv[win, HD:]
        q = q_h[h, rows, :]
        do = do_v[rows, cols]
        score = dot(key, q, NT) + bias[b]
        top = jnp.max(score, axis=0, keepdims=True)
        weight = jnp.exp2((score - top) * coef)
        prob = weight * (1.0 / jnp.sum(weight, axis=0, keepdims=True))
        low = prob.astype(BF16)
        o_t = dot(vT[:, win], low).astype(BF16)
        delta = jnp.sum(o_t.astype(F32) * doT[h, :, rows].astype(F32), axis=0, keepdims=True)
        dscore = (prob * (dot(value, do, NT) - delta)).astype(BF16)
        out_ref[rows, cols] = o_t.T
        dq_t = dot(kT[:, win], dscore) * factor
        joined[h // 2, rows, (h % 2) * HD : (h % 2 + 1) * HD] = dq_t.T.astype(BF16)
        acc[win, 0:HD] += dot(dscore, q)
        acc[win, HD:] += dot(low, do)

    def attend_head(h):
        def step(b, carry):
            attend(h, b)
            return carry

        lax.fori_loop(0, 2, step, 0)

    def share(chunk):
        here = joined.at[chunk]
        return (
            copies.start(here, joined_s.at[chunk], sib),
            copies.start(here, jz.at[0, chunk], z_peer[1]),
            copies.start(here, jz.at[2, chunk], z_peer[3]),
        )

    def share_far(chunk, got):
        got[1].wait_recv()
        got[2].wait_recv()
        top, low = slice(0, 256), slice(256, 512)
        return (
            copies.start(jz.at[0, chunk, top], jz.at[1, chunk, top], z_peer[1]),
            copies.start(jz.at[2, chunk, low], jz.at[1, chunk, low], z_peer[3]),
        )

    def lhs(ref, axis, there):
        if axis == "y":
            return ref[there].reshape(512, TOK)
        return ref[:, there].reshape(512, TOK)

    def product(chunk, axis, there):
        full = dot(lhs(xT.at[0], axis, there), joined[chunk])
        full = full + dot(lhs(xTs, axis, there), joined_s[chunk])
        return full.reshape(4, 128, 256)

    axes = {"y": (y, y_peer), "x": (x, x_peer)}
    order = (("y", "x"), ("y", "x"), ("x", "y"))

    def reduce_first(chunk):
        axis = order[chunk][0]
        here, peer = axes[axis]
        s2[chunk] = product(chunk, axis, (here + 2) % 4).astype(BF16)
        return (
            copies.start(s2.at[chunk, 0:2], r2p.at[chunk], peer[1]),
            copies.start(s2.at[chunk, 2:4], r2m.at[chunk], peer[3]),
        )

    def reduce_second(chunk, got):
        axis = order[chunk][0]
        here, peer = axes[axis]
        up = product(chunk, axis, (here + 1) % 4)
        got[0].wait_recv()
        sp[chunk, 0:2] = (up[0:2] + r2p[chunk].astype(F32)).astype(BF16)
        sp[chunk, 2:4] = up[2:4].astype(BF16)
        one = copies.start(sp.at[chunk], r1p.at[chunk], peer[1])
        down = product(chunk, axis, (here + 3) % 4)
        got[1].wait_recv()
        sm[chunk, 0:2] = down[0:2].astype(BF16)
        sm[chunk, 2:4] = (down[2:4] + r2m[chunk].astype(F32)).astype(BF16)
        return one, copies.start(sm.at[chunk], r1m.at[chunk], peer[3])

    def reduce_third(chunk, got):
        axis = order[chunk][0]
        here, _ = axes[axis]
        own = product(chunk, axis, here)
        got[0].wait_recv()
        got[1].wait_recv()
        t_f[chunk] = own + r1p[chunk].astype(F32) + r1m[chunk].astype(F32)
        here, peer = axes[order[chunk][1]]
        t2[chunk] = t_f[chunk, (here + 2) % 4].astype(BF16)
        return (
            copies.start(t2.at[chunk, 0:64], u2p.at[chunk], peer[1]),
            copies.start(t2.at[chunk, 64:128], u2m.at[chunk], peer[3]),
        )

    def reduce_fourth(chunk, got):
        here, peer = axes[order[chunk][1]]
        up = t_f[chunk, (here + 1) % 4]
        got[0].wait_recv()
        tp[chunk, 0:64] = (up[0:64] + u2p[chunk].astype(F32)).astype(BF16)
        tp[chunk, 64:128] = up[64:128].astype(BF16)
        one = copies.start(tp.at[chunk], u1p.at[chunk], peer[1])
        down = t_f[chunk, (here + 3) % 4]
        got[1].wait_recv()
        tm[chunk, 0:64] = down[0:64].astype(BF16)
        tm[chunk, 64:128] = (down[64:128] + u2m[chunk].astype(F32)).astype(BF16)
        return one, copies.start(tm.at[chunk], u1m.at[chunk], peer[3])

    def reduce_last(chunk, got):
        here, _ = axes[order[chunk][1]]
        got[0].wait_recv()
        got[1].wait_recv()
        return t_f[chunk, here] + u1p[chunk].astype(F32) + u1m[chunk].astype(F32)

    def add_own(chunk):
        rows = pl.multiple_of(z * 1024, 1024)
        cols = slice(chunk * 256, (chunk + 1) * 256)
        term = dot(joined[chunk], w_v[pl.ds(rows, 1024), cols], NT)
        if chunk == 0:
            ig_acc[...] = term
        else:
            ig_acc[...] += term

    def add_far(chunk, slot):
        cols = slice(chunk * 256, (chunk + 1) * 256)
        weights = wz[slot, :, :, :, cols].reshape(1024, 256)
        ig_acc[...] += dot(jz[slot, chunk], weights, NT)

    attend_head(0)
    attend_head(1)
    got0 = share(0)
    for got in wy_got:
        got.wait_recv()
    ws_got = copies.start(wz.at[:, :, k], wz.at[:, :, k], sib)
    x_got.wait_recv()

    attend_head(2)
    got0[0].wait_recv()
    ring0 = reduce_first(0)
    far0 = share_far(0, got0)
    attend_head(3)
    got1 = share(1)

    ones = lax.broadcasted_iota(jnp.int32, (1, 2 * HD), 1)
    scale = jnp.where(ones < HD, factor, 1.0)
    dkv_send[0] = (acc[0:512] * scale).astype(BF16)
    dkv_send[1] = (acc[1024:1536] * scale).astype(BF16)
    pair_a = copies.make(dkv_send.at[1], dkv_sib.at[0], sib)
    pair_b = copies.make(dkv_send.at[0], dkv_sib.at[1], sib)
    far_d = copies.make(dkv_send.at[0], dkv_sib.at[1], third)
    pair_a.start()

    @pl.when(k == 1)
    def _():
        pair_b.start()

    @pl.when(k == 0)
    def _():
        far_d.start()

    pair_a.wait_recv()

    @pl.when(k == 0)
    def _():
        pair_b.wait_recv()

    came = dkv_sib[1 - k].astype(F32)
    dkv_send[2] = (acc[512:1024] * scale + came).astype(BF16)
    near_d = copies.start(dkv_send.at[2], dkv_x, prv)

    ring0 = reduce_second(0, ring0)
    got1[0].wait_recv()
    ring1 = reduce_first(1)
    far1 = share_far(1, got1)
    add_own(0)
    add_own(1)
    near_d.wait_recv()

    @pl.when(k == 1)
    def _():
        far_d.wait_recv()

    total = acc[1536:2048] * scale + dkv_x[...].astype(F32)
    joined[2] = (total + dkv_sib[k].astype(F32)).astype(BF16)
    got2 = share(2)
    ring1 = reduce_second(1, ring1)
    got2[0].wait_recv()
    ring2 = reduce_first(2)
    ring0 = reduce_third(0, ring0)
    add_own(2)
    ws_got.wait_recv()
    add_far(0, 0)
    add_far(0, 2)
    far2 = share_far(2, got2)
    ring2 = reduce_second(2, ring2)
    ring0 = reduce_fourth(0, ring0)
    ring1 = reduce_third(1, ring1)
    far0[0].wait_recv()
    far0[1].wait_recv()
    add_far(0, 1)
    add_far(1, 0)
    add_far(1, 2)
    ring1 = reduce_fourth(1, ring1)
    ring2 = reduce_third(2, ring2)
    far1[0].wait_recv()
    far1[1].wait_recv()
    add_far(1, 1)
    add_far(2, 0)
    add_far(2, 2)
    ring2 = reduce_fourth(2, ring2)
    wqg_ref[:, 0:256] = reduce_last(0, ring0)
    wqg_ref[:, 256:512] = reduce_last(1, ring1)
    far2[0].wait_recv()
    far2[1].wait_recv()
    add_far(2, 1)
    ig_ref[...] = ig_acc[...].astype(BF16)
    last = reduce_last(2, ring2)
    wkg_ref[...] = last[:, 0:128]
    wvg_ref[...] = last[:, 128:256]

    for copy in copies.sent:
        copy.wait_send()
    pair_a.wait_send()

    @pl.when(k == 0)
    def _():
        kv2.wait_send()
        fwd0.wait_send()
        far_d.wait_send()

    @pl.when(k == 1)
    def _():
        kv0.wait_send()
        fwd2.wait_send()
        pair_b.wait_send()


def body(inputs, query_weight, key_weight, value_weight, out_grad, doc_lengths):
    any_space = pl.BlockSpec(memory_space=pl.ANY)
    vmem = pl.BlockSpec(memory_space=pltpu.VMEM)
    return pl.pallas_call(
        kernel,
        out_shape=(
            jax.ShapeDtypeStruct((TOK, 512), BF16),
            jax.ShapeDtypeStruct((TOK, 1024), BF16),
            jax.ShapeDtypeStruct((128, 512), F32),
            jax.ShapeDtypeStruct((128, 128), F32),
            jax.ShapeDtypeStruct((128, 128), F32),
        ),
        in_specs=[pl.BlockSpec(memory_space=pltpu.SMEM)] + [any_space] * 5,
        out_specs=(vmem,) * 5,
        scratch_shapes=[
            pltpu.VMEM((TOK, D), BF16),
            pltpu.VMEM((D, COLS), BF16),
            pltpu.VMEM((TOK, 512), BF16),
            pltpu.VMEM((2048, 256), BF16),
            pltpu.VMEM((HD, 2048), BF16),
            pltpu.VMEM((HD, 2048), BF16),
            pltpu.VMEM((GROUP, TOK, HD), BF16),
            pltpu.VMEM((GROUP, HD, TOK), BF16),
            pltpu.VMEM((2048, 256), F32),
            pltpu.VMEM((2, WIN, QB), F32),
            pltpu.VMEM((2, 4, 4, 128, TOK), BF16),
            pltpu.VMEM((4, 4, 128, TOK), BF16),
            pltpu.VMEM((3, 4, 2, 128, COLS), BF16),
            pltpu.VMEM((3, TOK, 256), BF16),
            pltpu.VMEM((3, TOK, 256), BF16),
            pltpu.VMEM((3, 3, TOK, 256), BF16),
            pltpu.VMEM((3, TOK, 256), BF16),
            pltpu.VMEM((2, TOK, 256), BF16),
            pltpu.VMEM((TOK, 256), BF16),
            pltpu.VMEM((3, 2, 128, 256), BF16),
            pltpu.VMEM((3, 2, 128, 256), BF16),
            pltpu.VMEM((3, 4, 128, 256), BF16),
            pltpu.VMEM((3, 4, 128, 256), BF16),
            pltpu.VMEM((3, 4, 128, 256), BF16),
            pltpu.VMEM((3, 4, 128, 256), BF16),
            pltpu.VMEM((3, 4, 128, 256), BF16),
            pltpu.VMEM((3, 4, 128, 256), F32),
            pltpu.VMEM((3, 64, 256), BF16),
            pltpu.VMEM((3, 64, 256), BF16),
            pltpu.VMEM((3, 128, 256), BF16),
            pltpu.VMEM((3, 128, 256), BF16),
            pltpu.VMEM((3, 128, 256), BF16),
            pltpu.VMEM((3, 128, 256), BF16),
            pltpu.VMEM((3, 128, 256), BF16),
            pltpu.VMEM((TOK, 1024), F32),
            pltpu.SemaphoreType.DMA((N_COPIES,)),
            pltpu.SemaphoreType.DMA((N_COPIES,)),
            pltpu.SemaphoreType.DMA((5,)),
        ],
        compiler_params=pltpu.CompilerParams(
            collective_id=0, has_side_effects=True, vmem_limit_bytes=63 * 2**20
        ),
        cost_estimate=pl.CostEstimate(
            flops=2 * 10**10, bytes_accessed=13 * 10**6, transcendentals=4 * 10**6
        ),
        name="attention_layer",
    )(doc_lengths, inputs, query_weight, key_weight, value_weight, out_grad)


def solution(mesh):
    return jax.shard_map(
        body,
        mesh=mesh,
        in_specs=(
            P("ctx", None),
            P(None, "head"),
            P(None, "head"),
            P(None, "head"),
            P("ctx", "head"),
            P(),
        ),
        out_specs=(P("ctx", "head"),) * 5,
        check_vma=False,
    )
```

time: 315 us -> 114 us (0.36); the launches traced: 309 us -> 113 us
  waiting for transfers between devices: 189 us -> 0 us
  Pallas kernels: 0 us -> 103 us
  matrix products: 43.9 us -> 0 us
  starting transfers between devices: 27.8 us -> 0 us
  between operations: 17.3 us -> 0.64 us
  local copies, waits for them, and re-layouts: 22.4 us -> 8.74 us
  other arithmetic: 7.23 us -> 0 us
    reduce_scatter x2 -> x0, waiting for transfers between devices: 170 us -> none  [the longest x1 125 us: body(): lax.psum_scatter(full_term, 'ctx', scatter_dimension=0, tiled=True)]
    pallas_call x0 -> x1, Pallas kernels: none -> 103 us  [body(): pl.pallas_call(kernel, out_shape=(jax.ShapeDtypeStruct((TOK, 512), BF16),...]
    dot_general x14 -> x0, matrix products: 43.9 us -> none  [the longest x1 9.18 us: body(): lax.dot_general(inputs, joined, (((0,), (0,)), ((), ())), preferred_eleme...]
    ppermute x12 -> x0, starting transfers between devices: 27.5 us -> none  [from_behind(): lax.ppermute(value, axis, [(source, source + steps) for source in range(i...]
    ppermute x12 -> x0, waiting for transfers between devices: 18.8 us -> none  [from_behind(): lax.ppermute(value, axis, [(source, source + steps) for source in range(i...]
    cond x21 -> x0, local copies, waits for them, and re-layouts: 11.6 us -> none  [the longest x8 9.87 us: body(): lax.cond(jnp.any(mask), grads_fn, keep_carry, (query_acc, key_grads[blk_i...]
    unnamed x32 -> x5, local copies, waits for them, and re-layouts: 6.06 us -> 8.74 us
  transfers between devices with their start and end apart: 14 -> 0, of which waited for: 5 -> 0; matrix products, arithmetic and copies ran while one was open for 12% -> 0% of each run, Pallas kernels for 0% -> 0%
where the time goes in v1:
time: 114 us; the launch traced here: 113 us
  Pallas kernels  103 us (90%)
  local copies, waits for them, and re-layouts  8.74 us (8%)
    pallas_call x1, Pallas kernels, body(): pl.pallas_call(kernel, out_shape=(jax.ShapeDtypeStruct((TOK, 512), BF16),...  103 us
    unnamed x5, local copies, waits for them, and re-layouts  8.74 us

profile of v1, /device:TPU:0, one launch (start us, length us, event | category | flops | bytes accessed | tf_op | source)
XLA Modules:
  0.0 112.5 jit_solution(14006803307083689364)
XLA Ops:
  0.6 103.1 %attention_layer.1 = (bf16[512,512]{1,0:T(8,128)(2,1)}, bf16[512,1024]{1,0:T(8,128)(2,1)}, f32[128,512]{1,0:T(8,128)}, f32[128,128]{1,0:T(8,128)}, f32[128,128]{1,0:T(8,128)}) custom-call(s32[32]{0:T(128)} %doc_ref.1, bf16[512,4096]{1,0:T(8,128)(2,1)} %x_hbm.1, bf16[4096,512]{1,0:T(8,128)(2,1)} %wq_hbm.1, bf16[4096,128]{1,0:T(8,128)(2,1)} %wk_hbm.1, ...), custom_call_target="tpu_custom_call" | custom-call | flops 20000000000 | bytes 13000000 | tf_op jit(solution)/shard_map/attention_layer/pallas_call | solution.py:431
  103.8 1.9 %copy.16 = bf16[512,512]{1,0:T(8,128)(2,1)} copy(bf16[512,512]{1,0:T(8,128)(2,1)} %get-tuple-element.10) | data formatting | bytes 1048576
  105.6 2.3 %copy.17 = bf16[512,1024]{1,0:T(8,128)(2,1)} copy(bf16[512,1024]{1,0:T(8,128)(2,1)} %get-tuple-element.11) | data formatting | bytes 2097152
  107.9 1.7 %copy.18 = f32[128,512]{1,0:T(8,128)} copy(f32[128,512]{1,0:T(8,128)} %get-tuple-element.12) | data formatting | bytes 524288
  109.6 1.5 %copy.19 = f32[128,128]{1,0:T(8,128)} copy(f32[128,128]{1,0:T(8,128)} %get-tuple-element.13) | data formatting | bytes 131072
  111.0 1.5 %copy.20 = f32[128,128]{1,0:T(8,128)} copy(f32[128,128]{1,0:T(8,128)} %get-tuple-element.14) | data formatting | bytes 131072

commit v2 on v1

v2 whole, which is shorter than its diff:
```python
import functools
import math

import jax
import jax.numpy as jnp
from jax import lax
from jax.experimental import pallas as pl
from jax.experimental.pallas import tpu as pltpu
from jax.sharding import PartitionSpec as P

HD = 128
GROUP = 4
TOK = 512
D = 4096
QB = 256
WIN = 1664
COLS = 768
NEG = -1e30
MESH = pl.DeviceIdType.MESH
F32 = jnp.float32
BF16 = jnp.bfloat16

NN = (((1,), (0,)), ((), ()))
NT = (((1,), (1,)), ((), ()))


def dot(a, b, dims=NN):
    return lax.dot_general(a, b, dims, preferred_element_type=F32)


class Copies:
    def __init__(self, send_sem, recv_sem):
        self.send_sem, self.recv_sem, self.used = send_sem, recv_sem, 0
        self.sent = []

    def make(self, src, dst, device):
        idx = self.used
        self.used += 1
        return pltpu.make_async_remote_copy(
            src_ref=src,
            dst_ref=dst,
            send_sem=self.send_sem.at[idx],
            recv_sem=self.recv_sem.at[idx],
            device_id=device,
            device_id_type=MESH,
        )

    def plan(self, src, dst, device):
        copy = self.make(src, dst, device)
        self.sent.append(copy)
        return copy

    def start(self, src, dst, device):
        copy = self.plan(src, dst, device)
        copy.start()
        return copy


N_COPIES = 100
TILE = 64
RING = 1


def sum_scratch(width, ring):
    half, whole = pltpu.VMEM((2, 128, width), BF16), pltpu.VMEM((4, 128, width), BF16)
    if ring:
        refs = {"r2p": half, "r2m": half, "r1p": whole, "r1m": whole, "s2": whole, "sp": whole, "sm": whole}
    else:
        blocks = pltpu.VMEM((3, 4, 128, width), BF16)
        refs = {"out1": blocks, "in1": blocks}
    rows = pltpu.VMEM((3, 128, width), BF16)
    return refs | {"out2": rows, "in2": rows, "t": pltpu.VMEM((4, 128, width), F32)}


def kernel(
    doc_ref, x_hbm, wq_hbm, wk_hbm, wv_hbm, do_hbm,
    out_ref, ig_ref, wqg_ref, wkg_ref, wvg_ref,
    x_v, w_v, do_v, kv, kT, vT, q_h, doT, acc, bias, xT, xTo, wz, joined, jz,
    dkv_send, dkv_sib, dkv_x, rings, pb, ig_acc, wg_v, s_f, p_f, low, dsc,
    send_sem, recv_sem, load_sem, store_sem,
):
    ctx = lax.axis_index("ctx")
    z = lax.axis_index("head")
    chip = ctx // 2
    k = ctx % 2
    y, x = chip // 4, chip % 4
    factor = HD ** -0.5

    def at(yy, xx, kk, zz):
        return ((yy % 4) * 8 + (xx % 4) * 2 + kk, zz % 4)

    def chip_at(pp, kk):
        return ((pp % 16) * 2 + kk, z)

    sib = at(y, x, 1 - k, z)
    z_peer = [None] + [at(y, x, k, z + r) for r in (1, 2, 3)]
    y_peer = [None] + [at(y + r, x, k, z) for r in (1, 2, 3)]
    x_peer = [None] + [at(y, x + r, k, z) for r in (1, 2, 3)]
    nxt, prv = chip_at(chip + 1, k), chip_at(chip + 15, k)
    third = chip_at(jnp.where(k == 1, chip + 2, chip + 14), 1 - k)

    loads = [
        pltpu.make_async_copy(wk_hbm, w_v.at[:, 512:640], load_sem.at[0]),
        pltpu.make_async_copy(wv_hbm, w_v.at[:, 640:768], load_sem.at[1]),
        pltpu.make_async_copy(x_hbm, x_v, load_sem.at[2]),
        pltpu.make_async_copy(wq_hbm, w_v.at[:, 0:512], load_sem.at[3]),
        pltpu.make_async_copy(do_hbm, do_v, load_sem.at[4]),
    ]
    for load in loads:
        load.start()

    barrier = pltpu.get_barrier_semaphore()
    partners = [sib, *z_peer[1:], *y_peer[1:], *x_peer[1:], nxt, prv, third]
    for partner in partners:
        pl.semaphore_signal(barrier, inc=1, device_id=partner, device_id_type=MESH)

    ig_v, out_v = x_v.at[:, 0:1024], x_v.at[:, 1024:1536]
    copies = Copies(send_sem, recv_sem)
    stores = []

    def store(src, dst):
        move = pltpu.make_async_copy(src, dst, store_sem.at[len(stores)])
        move.start()
        stores.append(move)

    for load in loads[:3]:
        load.wait()
    kv[1536:2048, :] = dot(x_v[...], w_v[:, 512:768]).astype(BF16)
    pl.semaphore_wait(barrier, len(partners))
    own_kv = kv.at[1536:2048]
    kv1 = copies.start(own_kv, kv.at[512:1024], nxt)
    kv2 = copies.make(own_kv, kv.at[1024:1536], sib)
    kv0a = copies.make(kv.at[1920:2048], kv.at[384:512], third)
    kv0b = copies.make(kv.at[1664:1920], kv.at[128:384], third)

    @pl.when(k == 0)
    def _():
        kv2.start()

    @pl.when(k == 1)
    def _():
        kv0a.start()

    def begin(*group):
        for copy in group:
            copy.start()

    def arrive(*group):
        for copy in group:
            copy.wait_recv()

    for load in loads[3:]:
        load.wait()

    wz_got = []
    for r in (1, 2, 3):
        for begins, rows, part in ((0, 32, y), (32, 96, x)):
            first_row = pl.multiple_of(((z + r) % 4) * 1024 + part * 256 + k * 128 + begins, 32)
            there = wz.at[r - 1, part, k, begins : begins + rows]
            wz_got.append(copies.start(w_v.at[pl.ds(first_row, rows), :], there, z_peer[r]))

    for h in range(0, GROUP, 2):
        both = dot(x_v[...], w_v[:, h * HD : (h + 2) * HD]).astype(BF16)
        q_h[h] = both[:, :HD]
        q_h[h + 1] = both[:, HD:]

    def transpose_x(i, carry):
        own = pl.multiple_of((2 * i + k) * 128, 128)
        other = pl.multiple_of((2 * i + 1 - k) * 128, 128)
        xT[i, :, 0:TOK] = x_v[:, pl.ds(own, 128)].T
        xTo[i] = x_v[:, pl.ds(other, 128)].T
        return carry

    lax.fori_loop(0, 16, transpose_x, 0)
    x_got = copies.start(xTo, xT.at[:, :, TOK : 2 * TOK], sib)

    for h in range(GROUP):
        doT[h] = do_v[:, h * HD : (h + 1) * HD].T

    pos = ctx * TOK + lax.broadcasted_iota(jnp.int32, (1, TOK), 1)
    start = jnp.zeros((1, TOK), jnp.int32)
    end = jnp.int32(0)
    for j in range(32):
        length = doc_ref[j]
        end = end + length
        start = start + jnp.where(pos >= end, length, 0)
    first = start - (ctx - 3) * TOK
    for b in range(2):
        key_pos = 128 + QB * b + lax.broadcasted_iota(jnp.int32, (WIN, QB), 0)
        query_pos = 1536 + QB * b + lax.broadcasted_iota(jnp.int32, (WIN, QB), 1)
        seen = (key_pos >= first[:, b * QB : (b + 1) * QB]) & (key_pos <= query_pos)
        bias[b] = jnp.where(seen, 0.0, NEG)
    acc[...] = jnp.zeros_like(acc)
    dkv_sib[1, 0:128] = jnp.zeros((128, 256), BF16)

    def transpose_kv(begin, stop):
        kT[:, begin:stop] = kv[begin:stop, 0:HD].T
        vT[:, begin:stop] = kv[begin:stop, HD:].T

    transpose_kv(1536, 2048)
    kv1.wait_recv()
    fwd2 = copies.make(kv.at[512:1024], kv.at[1024:1536], sib)
    fwd0 = copies.make(kv.at[640:1024], kv.at[128:512], sib)

    @pl.when(k == 0)
    def _():
        fwd0.start()

    @pl.when(k == 1)
    def _():
        fwd2.start()
        kv0b.start()

    transpose_kv(512, 1024)

    arrive(*wz_got)
    mine_y, mine_x = wz.at[:, y, k, 0:32], wz.at[:, x, k, 32:128]
    wy_got = [copies.start(mine_y, mine_y, y_peer[r]) for r in (1, 2, 3)]
    wx_got = [copies.start(mine_x, mine_x, x_peer[r]) for r in (1, 3)]
    left, right = wz.at[:, (x + 3) % 4, k, 32:80], wz.at[:, (x + 1) % 4, k, 80:128]
    wx_far = (copies.plan(left, left, x_peer[1]), copies.plan(right, right, x_peer[3]))

    @pl.when(k == 0)
    def _():
        fwd2.wait_recv()
        kv0a.wait_recv()

    @pl.when(k == 1)
    def _():
        kv2.wait_recv()
        fwd0.wait_recv()

    transpose_kv(384, 512)
    transpose_kv(1024, 1536)

    coef = factor * math.log2(math.e)

    def attend(hp, b):
        win = pl.ds(pl.multiple_of(128 + QB * b, 128), WIN)
        rows = pl.ds(pl.multiple_of(QB * b, QB), QB)
        at_a = pl.ds(pl.multiple_of(2 * hp * HD, HD), HD)
        at_b = pl.ds(pl.multiple_of((2 * hp + 1) * HD, HD), HD)
        q = jnp.concatenate([q_h[2 * hp, rows, :], q_h[2 * hp + 1, rows, :]], axis=0)
        do = jnp.concatenate([do_v[rows, at_a], do_v[rows, at_b]], axis=0)
        do_t = jnp.concatenate([doT[2 * hp, :, rows], doT[2 * hp + 1, :, rows]], axis=1)
        s_f[...] = dot(kv[win, 0:HD], q, NT)
        p_f[...] = dot(kv[win, HD:], do, NT)
        tiles = [slice(t, t + TILE) for t in range(0, WIN, TILE)]
        top = None
        for r in tiles:
            mask = bias[b, r]
            score = s_f[r] + jnp.concatenate([mask, mask], axis=1)
            s_f[r] = score
            most = jnp.max(score.reshape(TILE // 8, 8, 2 * QB), axis=0)
            top = most if top is None else jnp.maximum(top, most)
        top = jnp.max(top, axis=0, keepdims=True) * coef
        total = None
        for r in tiles:
            weight = jnp.exp2(s_f[r] * coef - top)
            s_f[r] = weight
            low[r] = weight.astype(BF16)
            part = jnp.sum(weight.reshape(TILE // 8, 8, 2 * QB), axis=0)
            total = part if total is None else total + part
        inverse = 1.0 / jnp.sum(total, axis=0, keepdims=True)
        o_t = (dot(vT[:, win], low[...]) * inverse).astype(BF16)
        delta = jnp.sum(o_t.astype(F32) * do_t.astype(F32), axis=0, keepdims=True)
        o = o_t.T
        out_v[rows, at_a] = o[:QB]
        out_v[rows, at_b] = o[QB:]
        for r in tiles:
            dsc[r] = (s_f[r] * (p_f[r] - delta)).astype(BF16)
        dq = (dot(kT[:, win], dsc[...]) * (inverse * factor)).T.astype(BF16)
        joined[rows, at_a] = dq[:QB]
        joined[rows, at_b] = dq[QB:]
        q_n = (q.T.astype(F32) * inverse).astype(BF16)
        do_n = (do_t.astype(F32) * inverse).astype(BF16)
        acc[win, 0:HD] += dot(dsc[...], q_n, NT)
        acc[win, HD:] += dot(low[...], do_n, NT)

    def columns(group):
        return slice(group * 256, (group + 1) * 256)

    def share(group, rows):
        here = joined.at[rows, columns(group)]
        return (
            copies.plan(here, jz.at[0, rows, columns(group)], z_peer[1]),
            copies.plan(here, jz.at[2, rows, columns(group)], z_peer[3]),
        )

    def share_core(group):
        cols = columns(group)
        return copies.plan(joined.at[0:TOK, cols], joined.at[TOK : 2 * TOK, cols], sib)

    def share_far(group, rows):
        cols, middle = columns(group), (rows.start + rows.stop) // 2
        above, below = slice(rows.start, middle), slice(middle, rows.stop)
        return (
            copies.plan(jz.at[0, above, cols], jz.at[1, above, cols], z_peer[1]),
            copies.plan(jz.at[2, below, cols], jz.at[1, below, cols], z_peer[3]),
        )

    axes = {"y": (y, y_peer), "x": (x, x_peer)}
    order = (("y", "x"), ("y", "x"), ("x", "y"), ("y", "x"))
    pieces = ((0, slice(0, 256)), (1, slice(0, 256)), (2, slice(0, 128)), (2, slice(128, 256)))

    def product(group):
        def rows_of(i, carry):
            part = xT[pl.ds(4 * i, 4)].reshape(512, 2 * TOK)
            pb[group, i] = dot(part, joined[:, columns(group)]).reshape(4, 128, 256)
            return carry

        lax.fori_loop(0, 4, rows_of, 0)

    def term(chunk, there):
        group, cols = pieces[chunk]
        if order[chunk][0] == "y":
            return pb[group, there, :, :, cols]
        return pb[group, :, there, :, cols]

    first_moves, second_moves = [], []
    for chunk in range(4):
        buf = rings[chunk]
        one, two = axes[order[chunk][0]][1], axes[order[chunk][1]][1]
        if chunk == RING:
            first_moves.append(
                (
                    copies.plan(buf["s2"].at[0:2], buf["r2p"], one[1]),
                    copies.plan(buf["s2"].at[2:4], buf["r2m"], one[3]),
                    copies.plan(buf["sp"], buf["r1p"], one[1]),
                    copies.plan(buf["sm"], buf["r1m"], one[3]),
                )
            )
        else:
            first_moves.append(
                [copies.plan(buf["out1"].at[r - 1], buf["in1"].at[r - 1], one[r]) for r in (1, 2, 3)]
            )
        second_moves.append(
            [copies.plan(buf["out2"].at[r - 1], buf["in2"].at[r - 1], two[r]) for r in (1, 2, 3)]
        )

    def send_first(chunk):
        here, _ = axes[order[chunk][0]]
        for r in (1, 2, 3):
            rings[chunk]["out1"][r - 1] = term(chunk, (here + r) % 4).astype(BF16)
        begin(*first_moves[chunk])

    def ring_first(chunk):
        here, _ = axes[order[chunk][0]]
        buf, moves = rings[chunk], first_moves[chunk]
        buf["s2"][...] = term(chunk, (here + 2) % 4).astype(BF16)
        begin(moves[0], moves[1])

    def ring_second(chunk):
        here, _ = axes[order[chunk][0]]
        buf, moves = rings[chunk], first_moves[chunk]
        up, down = term(chunk, (here + 1) % 4), term(chunk, (here + 3) % 4)
        buf["sp"][2:4] = up[2:4].astype(BF16)
        buf["sm"][0:2] = down[0:2].astype(BF16)
        arrive(moves[0])
        buf["sp"][0:2] = (up[0:2] + buf["r2p"][...].astype(F32)).astype(BF16)
        begin(moves[2])
        arrive(moves[1])
        buf["sm"][2:4] = (down[2:4] + buf["r2m"][...].astype(F32)).astype(BF16)
        begin(moves[3])

    def send_second(chunk):
        here, _ = axes[order[chunk][0]]
        buf = rings[chunk]
        if chunk == RING:
            arrive(first_moves[chunk][2], first_moves[chunk][3])
            sent = buf["r1p"][...].astype(F32) + buf["r1m"][...].astype(F32)
        else:
            arrive(*first_moves[chunk])
            sent = sum(buf["in1"][r].astype(F32) for r in range(3))
        buf["t"][...] = term(chunk, here) + sent
        here, _ = axes[order[chunk][1]]
        for r in (1, 2, 3):
            buf["out2"][r - 1] = buf["t"][(here + r) % 4].astype(BF16)
        begin(*second_moves[chunk])

    def finish(chunk):
        here, _ = axes[order[chunk][1]]
        buf = rings[chunk]
        arrive(*second_moves[chunk])
        group, cols = pieces[chunk]
        first_col = group * 256 + cols.start
        last = buf["t"][here] + sum(buf["in2"][r].astype(F32) for r in range(3))
        wg_v[:, first_col : first_col + last.shape[1]] = last

    def own_term(group):
        rows = pl.ds(pl.multiple_of(z * 1024, 1024), 1024)
        return dot(joined[0:TOK, columns(group)], w_v[rows, columns(group)], NT)

    def far_term(group, slot):
        weights = wz[slot, :, :, :, columns(group)].reshape(1024, 256)
        return dot(jz[slot, :, columns(group)], weights, NT)

    def add(value):
        ig_acc[...] += value

    ones = lax.broadcasted_iota(jnp.int32, (1, 2 * HD), 1)
    scale = jnp.where(ones < HD, factor, 1.0)
    above, below, every = slice(0, 256), slice(256, 512), slice(0, TOK)
    near01, near00 = share(0, below), share(0, above)
    near10, near11 = share(1, above), share(1, below)
    near2 = share(2, every)
    far01, far00 = share_far(0, below), share_far(0, above)
    far10, far11 = share_far(1, above), share_far(1, below)
    far2 = share_far(2, every)
    core = [share_core(group) for group in range(3)]
    ws_got = copies.plan(wz.at[:, :, k], wz.at[:, :, k], sib)

    pair_c = copies.make(dkv_send.at[0, 0:256], dkv_sib.at[1, 128:384], sib)
    far_c = copies.make(dkv_send.at[0, 0:256], dkv_sib.at[1, 128:384], third)
    pair_a = copies.plan(dkv_send.at[1], dkv_sib.at[0], sib)
    pair_b = copies.make(dkv_send.at[0, 256:384], dkv_sib.at[1, 384:512], sib)
    far_d = copies.make(dkv_send.at[0, 256:384], dkv_sib.at[1, 384:512], third)
    near_d = copies.plan(dkv_send.at[2], dkv_x, prv)

    def step(i, carry):
        attend(i // 2, ((i + 1) // 2 + 1) % 2)

        @pl.when(i == 0)
        def _():
            begin(*near01)

            @pl.when(k == 0)
            def _():
                kv0b.wait_recv()

            transpose_kv(128, 384)

        @pl.when(i == 1)
        def _():
            begin(*near00, core[0])
            arrive(*near01)
            begin(*far01)
            ig_acc[...] = own_term(0)
            arrive(x_got, core[0])
            product(0)
            send_first(0)
            arrive(*wx_got)
            begin(*wx_far)

        @pl.when(i == 2)
        def _():
            begin(*near10)
            dkv_send[0, 0:256] = (acc[128:384] * scale).astype(BF16)

            @pl.when(k == 1)
            def _():
                pair_c.start()

            @pl.when(k == 0)
            def _():
                far_c.start()

            arrive(*near00)
            begin(*far00)
            arrive(*wy_got, *wx_far)
            begin(ws_got)

        return carry

    lax.fori_loop(0, 4, step, 0)
    begin(*near11, core[1])
    dkv_send[0, 256:384] = (acc[384:512] * scale).astype(BF16)
    dkv_send[1] = (acc[1024:1536] * scale).astype(BF16)
    begin(pair_a)

    @pl.when(k == 1)
    def _():
        pair_b.start()

    @pl.when(k == 0)
    def _():
        far_d.start()

    store(out_v, out_ref)
    arrive(*near10)
    begin(*far10)
    add(own_term(1))
    arrive(pair_a)

    @pl.when(k == 0)
    def _():
        pair_b.wait_recv()
        pair_c.wait_recv()

    came = dkv_sib[1 - k].astype(F32)
    dkv_send[2] = (acc[512:1024] * scale + came).astype(BF16)
    begin(near_d)
    arrive(core[1])
    product(1)
    ring_first(1)
    arrive(ws_got)
    add(far_term(0, 0))
    add(far_term(0, 2))
    arrive(*near11)
    begin(*far11)
    arrive(*far00, *far01)
    add(far_term(0, 1))
    arrive(near_d)

    @pl.when(k == 1)
    def _():
        far_c.wait_recv()
        far_d.wait_recv()

    total = acc[1536:2048] * scale + dkv_x[...].astype(F32)
    joined[0:TOK, 512:768] = (total + dkv_sib[k].astype(F32)).astype(BF16)
    begin(*near2, core[2])
    ring_second(1)
    add(own_term(2))
    arrive(core[2])
    product(2)
    send_first(2)
    send_first(3)
    send_second(0)
    add(far_term(1, 0))
    add(far_term(1, 2))
    arrive(*far10, *far11)
    add(far_term(1, 1))
    arrive(*near2)
    begin(*far2)
    add(far_term(2, 0))
    add(far_term(2, 2))
    send_second(1)
    send_second(2)
    send_second(3)
    finish(0)
    arrive(*far2)
    ig_v[...] = (ig_acc[...] + far_term(2, 1)).astype(BF16)
    store(ig_v, ig_ref)
    finish(1)
    store(wg_v.at[:, 0:512], wqg_ref)
    finish(2)
    store(wg_v.at[:, 512:640], wkg_ref)
    finish(3)
    store(wg_v.at[:, 640:768], wvg_ref)

    for copy in copies.sent:
        copy.wait_send()

    @pl.when(k == 0)
    def _():
        kv2.wait_send()
        fwd0.wait_send()
        far_c.wait_send()
        far_d.wait_send()

    @pl.when(k == 1)
    def _():
        kv0a.wait_send()
        kv0b.wait_send()
        fwd2.wait_send()
        pair_b.wait_send()
        pair_c.wait_send()

    for move in stores:
        move.wait()


def hand_over(*refs):
    sources, targets, held, sem = refs[:5], refs[5:10], refs[10:15], refs[15]
    reads = [pltpu.make_async_copy(sources[i], held[i], sem.at[0, i]) for i in range(5)]
    writes = [pltpu.make_async_copy(held[i], targets[i], sem.at[1, i]) for i in range(5)]
    for read in reads:
        read.start()
    for read, write in zip(reads, writes):
        read.wait()
        write.start()
    for write in writes:
        write.wait()


def body(inputs, query_weight, key_weight, value_weight, out_grad, doc_lengths):
    any_space = pl.BlockSpec(memory_space=pl.ANY)
    shapes = (
        jax.ShapeDtypeStruct((TOK, 512), BF16),
        jax.ShapeDtypeStruct((TOK, 1024), BF16),
        jax.ShapeDtypeStruct((128, 512), F32),
        jax.ShapeDtypeStruct((128, 128), F32),
        jax.ShapeDtypeStruct((128, 128), F32),
    )
    results = pl.pallas_call(
        kernel,
        out_shape=shapes,
        in_specs=[pl.BlockSpec(memory_space=pltpu.SMEM)] + [any_space] * 5,
        out_specs=(any_space,) * 5,
        scratch_shapes=[
            pltpu.VMEM((TOK, D), BF16),
            pltpu.VMEM((D, COLS), BF16),
            pltpu.VMEM((TOK, 512), BF16),
            pltpu.VMEM((2048, 256), BF16),
            pltpu.VMEM((HD, 2048), BF16),
            pltpu.VMEM((HD, 2048), BF16),
            pltpu.VMEM((GROUP, TOK, HD), BF16),
            pltpu.VMEM((GROUP, HD, TOK), BF16),
            pltpu.VMEM((2048, 256), F32),
            pltpu.VMEM((2, WIN, QB), F32),
            pltpu.VMEM((16, 128, 2 * TOK), BF16),
            pltpu.VMEM((16, 128, TOK), BF16),
            pltpu.VMEM((3, 4, 2, 128, COLS), BF16),
            pltpu.VMEM((2 * TOK, COLS), BF16),
            pltpu.VMEM((3, TOK, COLS), BF16),
            pltpu.VMEM((3, TOK, 256), BF16),
            pltpu.VMEM((2, TOK, 256), BF16),
            pltpu.VMEM((TOK, 256), BF16),
            [sum_scratch(w, chunk == RING) for chunk, w in enumerate((256, 256, 128, 128))],
            pltpu.VMEM((3, 4, 4, 128, 256), F32),
            pltpu.VMEM((TOK, 1024), F32),
            pltpu.VMEM((128, COLS), F32),
            pltpu.VMEM((WIN, 2 * QB), F32),
            pltpu.VMEM((WIN, 2 * QB), F32),
            pltpu.VMEM((WIN, 2 * QB), BF16),
            pltpu.VMEM((WIN, 2 * QB), BF16),
            pltpu.SemaphoreType.DMA((N_COPIES,)),
            pltpu.SemaphoreType.DMA((N_COPIES,)),
            pltpu.SemaphoreType.DMA((5,)),
            pltpu.SemaphoreType.DMA((5,)),
        ],
        compiler_params=pltpu.CompilerParams(
            collective_id=0, has_side_effects=True, vmem_limit_bytes=63 * 2**20
        ),
        cost_estimate=pl.CostEstimate(
            flops=2 * 10**10, bytes_accessed=13 * 10**6, transcendentals=4 * 10**6
        ),
        name="attention_layer",
    )(doc_lengths, inputs, query_weight, key_weight, value_weight, out_grad)
    return pl.pallas_call(
        hand_over,
        out_shape=shapes,
        in_specs=[any_space] * 5,
        out_specs=(any_space,) * 5,
        scratch_shapes=[pltpu.VMEM(shape.shape, shape.dtype) for shape in shapes]
        + [pltpu.SemaphoreType.DMA((2, 5))],
        compiler_params=pltpu.CompilerParams(vmem_limit_bytes=63 * 2**20),
        name="hand_over",
    )(*results)


def solution(mesh):
    return jax.shard_map(
        body,
        mesh=mesh,
        in_specs=(
            P("ctx", None),
            P(None, "head"),
            P(None, "head"),
            P(None, "head"),
            P("ctx", "head"),
            P(),
        ),
        out_specs=(P("ctx", "head"),) * 5,
        check_vma=False,
    )
```

time: 114 us -> 79.4 us (0.70)
  Pallas kernels: 103 us -> 77.6 us
  local copies, waits for them, and re-layouts: 8.74 us -> 0 us
    pallas_call x1 -> x2, Pallas kernels: 103 us -> 77.6 us  [the longest x1 75.1 us: body(): pl.pallas_call(kernel, out_shape=shapes, in_specs=[pl.BlockSpec(memory_sp...]
    unnamed x5 -> x0, local copies, waits for them, and re-layouts: 8.74 us -> none
where the time goes in v2:
time: 79.4 us; the launch traced here: 78.4 us
  Pallas kernels  77.6 us (98%)
  between operations  0.8 us (1%)
    pallas_call x1, Pallas kernels, body(): pl.pallas_call(kernel, out_shape=shapes, in_specs=[pl.BlockSpec(memory_sp...  75.1 us
    pallas_call x1, Pallas kernels, body(): pl.pallas_call(hand_over, out_shape=shapes, in_specs=[any_space] * 5, out...  2.56 us

profile of v2, /device:TPU:0, one launch (start us, length us, event | category | flops | bytes accessed | tf_op | source)
XLA Modules:
  0.0 78.4 jit_solution(1096092930222314716)
XLA Ops:
  0.6 75.1 %attention_layer.1 = (bf16[512,512]{1,0:T(8,128)(2,1)}, bf16[512,1024]{1,0:T(8,128)(2,1)}, f32[128,512]{1,0:T(8,128)}, f32[128,128]{1,0:T(8,128)}, f32[128,128]{1,0:T(8,128)}) custom-call(s32[32]{0:T(128)} %doc_ref.1, bf16[512,4096]{1,0:T(8,128)(2,1)} %x_hbm.1, bf16[4096,512]{1,0:T(8,128)(2,1)} %wq_hbm.1, bf16[4096,128]{1,0:T(8,128)(2,1)} %wk_hbm.1, ...), custom_call_target="tpu_custom_call" | custom-call | flops 20000000000 | bytes 13000000 | tf_op jit(solution)/shard_map/attention_layer/pallas_call | solution.py:586
  75.7 2.6 %hand_over.1 = (bf16[512,512]{1,0:T(8,128)(2,1)}, bf16[512,1024]{1,0:T(8,128)(2,1)}, f32[128,512]{1,0:T(8,128)}, f32[128,128]{1,0:T(8,128)}, f32[128,128]{1,0:T(8,128)}) custom-call(bf16[512,512]{1,0:T(8,128)(2,1)} %get-tuple-element.10.refs_0_, bf16[512,1024]{1,0:T(8,128)(2,1)} %get-tuple-element.11.refs_1_, f32[128,512]{1,0:T(8,128)} %get-tuple-element.12.refs_2_, ...), custom_call_target="tpu_custom_call" | custom-call | tf_op jit(solution)/shard_map/hand_over/pallas_call | solution.py:631

commit v3 on v2

--- a/solution.py
+++ b/solution.py
@@ -58,13 +58,13 @@
 
 N_COPIES = 100
 TILE = 64
-RING = 1
+RINGS = (2, 3)
 
 
 def sum_scratch(width, ring):
-    half, whole = pltpu.VMEM((2, 128, width), BF16), pltpu.VMEM((4, 128, width), BF16)
+    whole = pltpu.VMEM((4, 128, width), BF16)
     if ring:
-        refs = {"r2p": half, "r2m": half, "r1p": whole, "r1m": whole, "s2": whole, "sp": whole, "sm": whole}
+        refs = {"r2": whole, "r1p": whole, "r1m": whole, "s2": whole, "sp": whole, "sm": whole}
     else:
         blocks = pltpu.VMEM((3, 4, 128, width), BF16)
         refs = {"out1": blocks, "in1": blocks}
@@ -154,8 +154,8 @@
 
     wz_got = []
     for r in (1, 2, 3):
-        for begins, rows, part in ((0, 32, y), (32, 96, x)):
-            first_row = pl.multiple_of(((z + r) % 4) * 1024 + part * 256 + k * 128 + begins, 32)
+        for begins, rows, part in ((0, 64, y), (64, 64, x)):
+            first_row = pl.multiple_of(((z + r) % 4) * 1024 + part * 256 + k * 128 + begins, 64)
             there = wz.at[r - 1, part, k, begins : begins + rows]
             wz_got.append(copies.start(w_v.at[pl.ds(first_row, rows), :], there, z_peer[r]))
 
@@ -214,11 +214,13 @@
     transpose_kv(512, 1024)
 
     arrive(*wz_got)
-    mine_y, mine_x = wz.at[:, y, k, 0:32], wz.at[:, x, k, 32:128]
-    wy_got = [copies.start(mine_y, mine_y, y_peer[r]) for r in (1, 2, 3)]
-    wx_got = [copies.start(mine_x, mine_x, x_peer[r]) for r in (1, 3)]
-    left, right = wz.at[:, (x + 3) % 4, k, 32:80], wz.at[:, (x + 1) % 4, k, 80:128]
-    wx_far = (copies.plan(left, left, x_peer[1]), copies.plan(right, right, x_peer[3]))
+    w_near, w_far = [], []
+    for begins, part, peer in ((0, y, y_peer), (64, x, x_peer)):
+        mine = wz.at[:, part, k, begins : begins + 64]
+        w_near += [copies.start(mine, mine, peer[r]) for r in (1, 3)]
+        down = wz.at[:, (part + 3) % 4, k, begins : begins + 32]
+        up = wz.at[:, (part + 1) % 4, k, begins + 32 : begins + 64]
+        w_far += [copies.plan(down, down, peer[1]), copies.plan(up, up, peer[3])]
 
     @pl.when(k == 0)
     def _():
@@ -300,8 +302,17 @@
         )
 
     axes = {"y": (y, y_peer), "x": (x, x_peer)}
-    order = (("y", "x"), ("y", "x"), ("x", "y"), ("y", "x"))
-    pieces = ((0, slice(0, 256)), (1, slice(0, 256)), (2, slice(0, 128)), (2, slice(128, 256)))
+    order = (("x", "y"), ("y", "x")) * 3
+    pieces = [(chunk // 2, slice(chunk % 2 * 128, (chunk % 2 + 1) * 128)) for chunk in range(6)]
+
+    def product_half(group, begins):
+        def rows_of(i, carry):
+            part = xT[pl.ds(4 * i, 4), :, begins : begins + TOK].reshape(512, TOK)
+            whole = dot(part, joined[begins : begins + TOK, columns(group)]).reshape(4, 128, 256)
+            pb[group, i] = whole if begins == 0 else pb[group, i] + whole
+            return carry
+
+        lax.fori_loop(0, 4, rows_of, 0)
 
     def product(group):
         def rows_of(i, carry):
@@ -318,14 +329,13 @@
         return pb[group, :, there, :, cols]
 
     first_moves, second_moves = [], []
-    for chunk in range(4):
+    for chunk in range(6):
         buf = rings[chunk]
         one, two = axes[order[chunk][0]][1], axes[order[chunk][1]][1]
-        if chunk == RING:
+        if chunk in RINGS:
             first_moves.append(
                 (
-                    copies.plan(buf["s2"].at[0:2], buf["r2p"], one[1]),
-                    copies.plan(buf["s2"].at[2:4], buf["r2m"], one[3]),
+                    copies.plan(buf["s2"], buf["r2"], one[1]),
                     copies.plan(buf["sp"], buf["r1p"], one[1]),
                     copies.plan(buf["sm"], buf["r1m"], one[3]),
                 )
@@ -346,28 +356,27 @@
 
     def ring_first(chunk):
         here, _ = axes[order[chunk][0]]
-        buf, moves = rings[chunk], first_moves[chunk]
+        buf = rings[chunk]
         buf["s2"][...] = term(chunk, (here + 2) % 4).astype(BF16)
-        begin(moves[0], moves[1])
-
-    def ring_second(chunk):
+        begin(first_moves[chunk][0])
+        buf["sm"][...] = term(chunk, (here + 3) % 4).astype(BF16)
+
+    def ring_down(chunk):
+        begin(first_moves[chunk][2])
+
+    def ring_up(chunk):
         here, _ = axes[order[chunk][0]]
-        buf, moves = rings[chunk], first_moves[chunk]
-        up, down = term(chunk, (here + 1) % 4), term(chunk, (here + 3) % 4)
-        buf["sp"][2:4] = up[2:4].astype(BF16)
-        buf["sm"][0:2] = down[0:2].astype(BF16)
-        arrive(moves[0])
-        buf["sp"][0:2] = (up[0:2] + buf["r2p"][...].astype(F32)).astype(BF16)
-        begin(moves[2])
-        arrive(moves[1])
-        buf["sm"][2:4] = (down[2:4] + buf["r2m"][...].astype(F32)).astype(BF16)
-        begin(moves[3])
+        buf = rings[chunk]
+        up = term(chunk, (here + 1) % 4)
+        arrive(first_moves[chunk][0])
+        buf["sp"][...] = (up + buf["r2"][...].astype(F32)).astype(BF16)
+        begin(first_moves[chunk][1])
 
     def send_second(chunk):
         here, _ = axes[order[chunk][0]]
         buf = rings[chunk]
-        if chunk == RING:
-            arrive(first_moves[chunk][2], first_moves[chunk][3])
+        if chunk in RINGS:
+            arrive(first_moves[chunk][1], first_moves[chunk][2])
             sent = buf["r1p"][...].astype(F32) + buf["r1m"][...].astype(F32)
         else:
             arrive(*first_moves[chunk])
@@ -436,11 +445,12 @@
             arrive(*near01)
             begin(*far01)
             ig_acc[...] = own_term(0)
+            arrive(*w_near)
+            begin(*w_far)
             arrive(x_got, core[0])
             product(0)
             send_first(0)
-            arrive(*wx_got)
-            begin(*wx_far)
+            send_first(1)
 
         @pl.when(i == 2)
         def _():
@@ -457,16 +467,13 @@
 
             arrive(*near00)
             begin(*far00)
-            arrive(*wy_got, *wx_far)
-            begin(ws_got)
 
         return carry
 
     lax.fori_loop(0, 4, step, 0)
-    begin(*near11, core[1])
-    dkv_send[0, 256:384] = (acc[384:512] * scale).astype(BF16)
     dkv_send[1] = (acc[1024:1536] * scale).astype(BF16)
     begin(pair_a)
+    dkv_send[0, 256:384] = (acc[384:512] * scale).astype(BF16)
 
     @pl.when(k == 1)
     def _():
@@ -476,67 +483,79 @@
     def _():
         far_d.start()
 
+    begin(*near11, core[1])
+    add(own_term(1))
+    arrive(pair_a)
+
+    @pl.when(k == 0)
+    def _():
+        pair_b.wait_recv()
+        pair_c.wait_recv()
+
+    came = dkv_sib[1 - k].astype(F32)
+    dkv_send[2] = (acc[512:1024] * scale + came).astype(BF16)
+    begin(near_d)
     store(out_v, out_ref)
     arrive(*near10)
     begin(*far10)
-    add(own_term(1))
-    arrive(pair_a)
-
-    @pl.when(k == 0)
-    def _():
-        pair_b.wait_recv()
-        pair_c.wait_recv()
-
-    came = dkv_sib[1 - k].astype(F32)
-    dkv_send[2] = (acc[512:1024] * scale + came).astype(BF16)
-    begin(near_d)
     arrive(core[1])
     product(1)
-    ring_first(1)
+    ring_first(2)
+    ring_first(3)
+    send_second(0)
+    send_second(1)
+    arrive(*near11)
+    begin(*far11)
+    arrive(*w_far)
+    begin(ws_got)
+    ring_up(2)
+    ring_up(3)
+    arrive(near_d)
+
+    @pl.when(k == 1)
+    def _():
+        far_c.wait_recv()
+        far_d.wait_recv()
+
+    total = acc[1536:2048] * scale + dkv_x[...].astype(F32)
+    joined[0:TOK, 512:768] = (total + dkv_sib[k].astype(F32)).astype(BF16)
+    begin(core[2], *near2)
+    ring_down(2)
+    ring_down(3)
+    product_half(2, 0)
+    arrive(core[2])
+    product_half(2, TOK)
+    send_first(4)
+    send_first(5)
+    add(own_term(2))
     arrive(ws_got)
     add(far_term(0, 0))
     add(far_term(0, 2))
-    arrive(*near11)
-    begin(*far11)
+    send_second(2)
+    send_second(3)
     arrive(*far00, *far01)
     add(far_term(0, 1))
-    arrive(near_d)
-
-    @pl.when(k == 1)
-    def _():
-        far_c.wait_recv()
-        far_d.wait_recv()
-
-    total = acc[1536:2048] * scale + dkv_x[...].astype(F32)
-    joined[0:TOK, 512:768] = (total + dkv_sib[k].astype(F32)).astype(BF16)
-    begin(*near2, core[2])
-    ring_second(1)
-    add(own_term(2))
-    arrive(core[2])
-    product(2)
-    send_first(2)
-    send_first(3)
-    send_second(0)
     add(far_term(1, 0))
+    arrive(*near2)
+    begin(*far2)
     add(far_term(1, 2))
     arrive(*far10, *far11)
     add(far_term(1, 1))
-    arrive(*near2)
-    begin(*far2)
     add(far_term(2, 0))
     add(far_term(2, 2))
-    send_second(1)
-    send_second(2)
-    send_second(3)
     finish(0)
+    finish(1)
+    send_second(4)
+    send_second(5)
+    finish(2)
+    finish(3)
+    store(wg_v.at[:, 0:512], wqg_ref)
     arrive(*far2)
     ig_v[...] = (ig_acc[...] + far_term(2, 1)).astype(BF16)
     store(ig_v, ig_ref)
-    finish(1)
-    store(wg_v.at[:, 0:512], wqg_ref)
-    finish(2)
+    finish(4)
     store(wg_v.at[:, 512:640], wkg_ref)
-    finish(3)
+    finish(5)
     store(wg_v.at[:, 640:768], wvg_ref)
 
     for copy in copies.sent:
@@ -607,7 +626,7 @@
             pltpu.VMEM((3, TOK, 256), BF16),
             pltpu.VMEM((2, TOK, 256), BF16),
             pltpu.VMEM((TOK, 256), BF16),
-            [sum_scratch(w, chunk == RING) for chunk, w in enumerate((256, 256, 128, 128))],
+            [sum_scratch(128, chunk in RINGS) for chunk in range(6)],
             pltpu.VMEM((3, 4, 4, 128, 256), F32),
             pltpu.VMEM((TOK, 1024), F32),
             pltpu.VMEM((128, COLS), F32),

time: 79.4 us -> 72.2 us (0.909); the launches traced: 78.4 us -> 72.1 us
  Pallas kernels: 77.6 us -> 71.3 us
    pallas_call x1, Pallas kernels: 75.1 us -> 68.7 us  [body(): pl.pallas_call(kernel, out_shape=shapes, in_specs=[pl.BlockSpec(memory_sp...]
where the time goes in v3:
time: 72.2 us; the launch traced here: 72.1 us
  Pallas kernels  71.3 us (99%)
  between operations  0.8 us (1%)
    pallas_call x1, Pallas kernels, body(): pl.pallas_call(kernel, out_shape=shapes, in_specs=[pl.BlockSpec(memory_sp...  68.7 us
    pallas_call x1, Pallas kernels, body(): pl.pallas_call(hand_over, out_shape=shapes, in_specs=[any_space] * 5, out...  2.56 us

profile of v3, /device:TPU:0, one launch (start us, length us, event | category | flops | bytes accessed | tf_op | source)
XLA Modules:
  0.0 72.1 jit_solution(11195477032023275071)
XLA Ops:
  0.6 68.7 %attention_layer.1 = (bf16[512,512]{1,0:T(8,128)(2,1)}, bf16[512,1024]{1,0:T(8,128)(2,1)}, f32[128,512]{1,0:T(8,128)}, f32[128,128]{1,0:T(8,128)}, f32[128,128]{1,0:T(8,128)}) custom-call(s32[32]{0:T(128)} %doc_ref.1, bf16[512,4096]{1,0:T(8,128)(2,1)} %x_hbm.1, bf16[4096,512]{1,0:T(8,128)(2,1)} %wq_hbm.1, bf16[4096,128]{1,0:T(8,128)(2,1)} %wk_hbm.1, ...), custom_call_target="tpu_custom_call" | custom-call | flops 20000000000 | bytes 13000000 | tf_op jit(solution)/shard_map/attention_layer/pallas_call | solution.py:605
  69.4 2.6 %hand_over.1 = (bf16[512,512]{1,0:T(8,128)(2,1)}, bf16[512,1024]{1,0:T(8,128)(2,1)}, f32[128,512]{1,0:T(8,128)}, f32[128,128]{1,0:T(8,128)}, f32[128,128]{1,0:T(8,128)}) custom-call(bf16[512,512]{1,0:T(8,128)(2,1)} %get-tuple-element.10.refs_0_, bf16[512,1024]{1,0:T(8,128)(2,1)} %get-tuple-element.11.refs_1_, f32[128,512]{1,0:T(8,128)} %get-tuple-element.12.refs_2_, ...), custom_call_target="tpu_custom_call" | custom-call | tf_op jit(solution)/shard_map/hand_over/pallas_call | solution.py:650

commit v4 on v3

--- a/solution.py
+++ b/solution.py
@@ -120,26 +120,46 @@
 
     def store(src, dst):
         move = pltpu.make_async_copy(src, dst, store_sem.at[len(stores)])
-        move.start()
         stores.append(move)
+        return move
+
+    out_store = store(out_v, out_ref)
+    ig_store = [store(ig_v, ig_ref)]
+    q_store = store(wg_v.at[:, 0:512], wqg_ref)
+    kv_store = [store(wg_v.at[:, 512:640], wkg_ref), store(wg_v.at[:, 640:768], wvg_ref)]
 
     for load in loads[:3]:
         load.wait()
     kv[1536:2048, :] = dot(x_v[...], w_v[:, 512:768]).astype(BF16)
     pl.semaphore_wait(barrier, len(partners))
     own_kv = kv.at[1536:2048]
-    kv1 = copies.start(own_kv, kv.at[512:1024], nxt)
+    kv1 = copies.make(own_kv, kv.at[512:1024], nxt)
     kv2 = copies.make(own_kv, kv.at[1024:1536], sib)
     kv0a = copies.make(kv.at[1920:2048], kv.at[384:512], third)
     kv0b = copies.make(kv.at[1664:1920], kv.at[128:384], third)
 
+    has_prv, has_nxt = chip >= 1, chip <= 14
+    gets_third, gives_third = (k == 0) & (chip >= 2), (k == 1) & (chip <= 13)
+
+    @pl.when(has_nxt)
+    def _():
+        kv1.start()
+
     @pl.when(k == 0)
     def _():
         kv2.start()
 
-    @pl.when(k == 1)
+    @pl.when(gives_third)
     def _():
         kv0a.start()
+
+    @pl.when(jnp.logical_not(has_prv))
+    def _():
+        kv[512:1024, :] = jnp.zeros((512, 256), BF16)
+
+    @pl.when((k == 0) & (chip <= 1))
+    def _():
+        kv[128:512, :] = jnp.zeros((384, 256), BF16)
 
     def begin(*group):
         for copy in group:
@@ -193,12 +213,24 @@
     acc[...] = jnp.zeros_like(acc)
     dkv_sib[1, 0:128] = jnp.zeros((128, 256), BF16)
 
+    @pl.when((k == 1) & (chip >= 14))
+    def _():
+        dkv_sib[1, 128:512] = jnp.zeros((384, 256), BF16)
+
+    @pl.when(jnp.logical_not(has_nxt))
+    def _():
+        dkv_x[...] = jnp.zeros((TOK, 256), BF16)
+
     def transpose_kv(begin, stop):
         kT[:, begin:stop] = kv[begin:stop, 0:HD].T
         vT[:, begin:stop] = kv[begin:stop, HD:].T
 
     transpose_kv(1536, 2048)
-    kv1.wait_recv()
+
+    @pl.when(has_prv)
+    def _():
+        kv1.wait_recv()
+
     fwd2 = copies.make(kv.at[512:1024], kv.at[1024:1536], sib)
     fwd0 = copies.make(kv.at[640:1024], kv.at[128:512], sib)
 
@@ -209,6 +241,9 @@
     @pl.when(k == 1)
     def _():
         fwd2.start()
+
+    @pl.when(gives_third)
+    def _():
         kv0b.start()
 
     transpose_kv(512, 1024)
@@ -225,6 +260,9 @@
     @pl.when(k == 0)
     def _():
         fwd2.wait_recv()
+
+    @pl.when(gets_third)
+    def _():
         kv0a.wait_recv()
 
     @pl.when(k == 1)
@@ -424,7 +462,7 @@
     pair_a = copies.plan(dkv_send.at[1], dkv_sib.at[0], sib)
     pair_b = copies.make(dkv_send.at[0, 256:384], dkv_sib.at[1, 384:512], sib)
     far_d = copies.make(dkv_send.at[0, 256:384], dkv_sib.at[1, 384:512], third)
-    near_d = copies.plan(dkv_send.at[2], dkv_x, prv)
+    near_d = copies.make(dkv_send.at[2], dkv_x, prv)
 
     def step(i, carry):
         attend(i // 2, ((i + 1) // 2 + 1) % 2)
@@ -433,7 +471,7 @@
         def _():
             begin(*near01)
 
-            @pl.when(k == 0)
+            @pl.when(gets_third)
             def _():
                 kv0b.wait_recv()
 
@@ -444,11 +482,11 @@
             begin(*near00, core[0])
             arrive(*near01)
             begin(*far01)
-            ig_acc[...] = own_term(0)
             arrive(*w_near)
             begin(*w_far)
             arrive(x_got, core[0])
-            product(0)
+            whole = dot(xT[...].reshape(2048, 2 * TOK), joined[:, columns(0)])
+            pb[0] = whole.reshape(4, 4, 128, 256)
             send_first(0)
             send_first(1)
 
@@ -461,7 +499,7 @@
             def _():
                 pair_c.start()
 
-            @pl.when(k == 0)
+            @pl.when(gets_third)
             def _():
                 far_c.start()
 
@@ -479,12 +517,12 @@
     def _():
         pair_b.start()
 
-    @pl.when(k == 0)
+    @pl.when(gets_third)
     def _():
         far_d.start()
 
     begin(*near11, core[1])
-    add(own_term(1))
+    ig_acc[...] = own_term(0)
     arrive(pair_a)
 
     @pl.when(k == 0)
@@ -494,25 +532,33 @@
 
     came = dkv_sib[1 - k].astype(F32)
     dkv_send[2] = (acc[512:1024] * scale + came).astype(BF16)
-    begin(near_d)
-    store(out_v, out_ref)
+
+    @pl.when(has_prv)
+    def _():
+        near_d.start()
+
+    begin(out_store)
     arrive(*near10)
     begin(*far10)
     arrive(core[1])
     product(1)
     ring_first(2)
     ring_first(3)
-    send_second(0)
-    send_second(1)
+    add(own_term(1))
     arrive(*near11)
     begin(*far11)
     arrive(*w_far)
     begin(ws_got)
     ring_up(2)
     ring_up(3)
-    arrive(near_d)
-
-    @pl.when(k == 1)
+    send_second(0)
+    send_second(1)
+
+    @pl.when(has_nxt)
+    def _():
+        near_d.wait_recv()
+
+    @pl.when(gives_third)
     def _():
         far_c.wait_recv()
         far_d.wait_recv()
@@ -531,8 +577,6 @@
     arrive(ws_got)
     add(far_term(0, 0))
     add(far_term(0, 2))
-    send_second(2)
-    send_second(3)
     arrive(*far00, *far01)
     add(far_term(0, 1))
     add(far_term(1, 0))
@@ -547,43 +591,65 @@
     finish(1)
     send_second(4)
     send_second(5)
+    send_second(2)
+    send_second(3)
+    arrive(*far2)
+    ig_v[...] = (ig_acc[...] + far_term(2, 1)).astype(BF16)
+    begin(*ig_store)
+    finish(4)
+    finish(5)
+    begin(*kv_store)
     finish(2)
     finish(3)
-    store(wg_v.at[:, 0:512], wqg_ref)
-    arrive(*far2)
-    ig_v[...] = (ig_acc[...] + far_term(2, 1)).astype(BF16)
-    store(ig_v, ig_ref)
-    finish(4)
-    store(wg_v.at[:, 512:640], wkg_ref)
-    finish(5)
-    store(wg_v.at[:, 640:768], wvg_ref)
+    begin(q_store)
 
     for copy in copies.sent:
         copy.wait_send()
 
+    @pl.when(has_nxt)
+    def _():
+        kv1.wait_send()
+
+    @pl.when(has_prv)
+    def _():
+        near_d.wait_send()
+
     @pl.when(k == 0)
     def _():
         kv2.wait_send()
         fwd0.wait_send()
-        far_c.wait_send()
-        far_d.wait_send()
 
     @pl.when(k == 1)
     def _():
-        kv0a.wait_send()
-        kv0b.wait_send()
         fwd2.wait_send()
         pair_b.wait_send()
         pair_c.wait_send()
 
+    @pl.when(gets_third)
+    def _():
+        far_c.wait_send()
+        far_d.wait_send()
+
+    @pl.when(gives_third)
+    def _():
+        kv0a.wait_send()
+        kv0b.wait_send()
+
     for move in stores:
         move.wait()
 
 
 def hand_over(*refs):
     sources, targets, held, sem = refs[:5], refs[5:10], refs[10:15], refs[15]
-    reads = [pltpu.make_async_copy(sources[i], held[i], sem.at[0, i]) for i in range(5)]
-    writes = [pltpu.make_async_copy(held[i], targets[i], sem.at[1, i]) for i in range(5)]
+    parts = [(i, slice(r, r + 128)) for i in range(5) for r in range(0, held[i].shape[0], 128)]
+    reads = [
+        pltpu.make_async_copy(sources[i].at[rows], held[i].at[rows], sem.at[0, n])
+        for n, (i, rows) in enumerate(parts)
+    ]
+    writes = [
+        pltpu.make_async_copy(held[i].at[rows], targets[i].at[rows], sem.at[1, n])
+        for n, (i, rows) in enumerate(parts)
+    ]
     for read in reads:
         read.start()
     for read, write in zip(reads, writes):
@@ -653,7 +719,7 @@
         in_specs=[any_space] * 5,
         out_specs=(any_space,) * 5,
         scratch_shapes=[pltpu.VMEM(shape.shape, shape.dtype) for shape in shapes]
-        + [pltpu.SemaphoreType.DMA((2, 5))],
+        + [pltpu.SemaphoreType.DMA((2, 11))],
         compiler_params=pltpu.CompilerParams(vmem_limit_bytes=63 * 2**20),
         name="hand_over",
     )(*results)

time: 72.2 us -> 71 us (0.983)
  Pallas kernels: 71.3 us -> 69.8 us
    pallas_call x1, Pallas kernels: 68.7 us -> 67.4 us  [body(): pl.pallas_call(kernel, out_shape=shapes, in_specs=[pl.BlockSpec(memory_sp...]
where the time goes in v4:
time: 71 us; the launch traced here: 70.6 us
  Pallas kernels  69.8 us (98%)
  between operations  0.8 us (1%)
    pallas_call x1, Pallas kernels, body(): pl.pallas_call(kernel, out_shape=shapes, in_specs=[pl.BlockSpec(memory_sp...  67.4 us
    pallas_call x1, Pallas kernels, body(): pl.pallas_call(hand_over, out_shape=shapes, in_specs=[any_space] * 5, out...  2.49 us

profile of v4, /device:TPU:0, one launch (start us, length us, event | category | flops | bytes accessed | tf_op | source)
XLA Modules:
  0.0 70.6 jit_solution(1616987403722913729)
XLA Ops:
  0.6 67.4 %attention_layer.1 = (bf16[512,512]{1,0:T(8,128)(2,1)}, bf16[512,1024]{1,0:T(8,128)(2,1)}, f32[128,512]{1,0:T(8,128)}, f32[128,128]{1,0:T(8,128)}, f32[128,128]{1,0:T(8,128)}) custom-call(s32[32]{0:T(128)} %doc_ref.1, bf16[512,4096]{1,0:T(8,128)(2,1)} %x_hbm.1, bf16[4096,512]{1,0:T(8,128)(2,1)} %wq_hbm.1, bf16[4096,128]{1,0:T(8,128)(2,1)} %wk_hbm.1, ...), custom_call_target="tpu_custom_call" | custom-call | flops 20000000000 | bytes 13000000 | tf_op jit(solution)/shard_map/attention_layer/pallas_call | solution.py:671
  68.0 2.5 %hand_over.1 = (bf16[512,512]{1,0:T(8,128)(2,1)}, bf16[512,1024]{1,0:T(8,128)(2,1)}, f32[128,512]{1,0:T(8,128)}, f32[128,128]{1,0:T(8,128)}, f32[128,128]{1,0:T(8,128)}) custom-call(bf16[512,512]{1,0:T(8,128)(2,1)} %get-tuple-element.10.refs_0_, bf16[512,1024]{1,0:T(8,128)(2,1)} %get-tuple-element.11.refs_1_, f32[128,512]{1,0:T(8,128)} %get-tuple-element.12.refs_2_, ...), custom_call_target="tpu_custom_call" | custom-call | tf_op jit(solution)/shard_map/hand_over/pallas_call | solution.py:716

commit v5 on v4

--- a/solution.py
+++ b/solution.py
@@ -56,7 +56,7 @@
         return copy
 
 
-N_COPIES = 100
+N_COPIES = 120
 TILE = 64
 RINGS = (2, 3)
 
@@ -128,10 +128,18 @@
     q_store = store(wg_v.at[:, 0:512], wqg_ref)
     kv_store = [store(wg_v.at[:, 512:640], wkg_ref), store(wg_v.at[:, 640:768], wvg_ref)]
 
+    pl.semaphore_wait(barrier, len(partners))
+    wz_got = []
+    for r in (1, 2, 3):
+        for begins, part in ((0, y), (64, x)):
+            row = pl.multiple_of(((z + r) % 4) * 1024 + part * 256 + k * 128 + begins, 64)
+            there = wz.at[r - 1, part, k, begins : begins + 64]
+            for weight, cols in ((wq_hbm, slice(0, 512)), (wk_hbm, slice(512, 640)), (wv_hbm, slice(640, 768))):
+                wz_got.append(copies.start(weight.at[pl.ds(row, 64), :], there.at[:, cols], z_peer[r]))
+
     for load in loads[:3]:
         load.wait()
     kv[1536:2048, :] = dot(x_v[...], w_v[:, 512:768]).astype(BF16)
-    pl.semaphore_wait(barrier, len(partners))
     own_kv = kv.at[1536:2048]
     kv1 = copies.make(own_kv, kv.at[512:1024], nxt)
     kv2 = copies.make(own_kv, kv.at[1024:1536], sib)
@@ -171,13 +179,6 @@
 
     for load in loads[3:]:
         load.wait()
-
-    wz_got = []
-    for r in (1, 2, 3):
-        for begins, rows, part in ((0, 64, y), (64, 64, x)):
-            first_row = pl.multiple_of(((z + r) % 4) * 1024 + part * 256 + k * 128 + begins, 64)
-            there = wz.at[r - 1, part, k, begins : begins + rows]
-            wz_got.append(copies.start(w_v.at[pl.ds(first_row, rows), :], there, z_peer[r]))
 
     for h in range(0, GROUP, 2):
         both = dot(x_v[...], w_v[:, h * HD : (h + 2) * HD]).astype(BF16)
@@ -580,6 +581,8 @@
     arrive(*far00, *far01)
     add(far_term(0, 1))
     add(far_term(1, 0))
+    send_second(2)
+    send_second(3)
     arrive(*near2)
     begin(*far2)
     add(far_term(1, 2))
@@ -591,17 +594,15 @@
     finish(1)
     send_second(4)
     send_second(5)
-    send_second(2)
-    send_second(3)
     arrive(*far2)
     ig_v[...] = (ig_acc[...] + far_term(2, 1)).astype(BF16)
     begin(*ig_store)
+    finish(2)
+    finish(3)
+    begin(q_store)
     finish(4)
     finish(5)
     begin(*kv_store)
-    finish(2)
-    finish(3)
-    begin(q_store)
 
     for copy in copies.sent:
         copy.wait_send()

time: 71 us -> 70.5 us (level)
  no operation moved by 1% of the time
where the time goes in v5:
time: 70.5 us; the launch traced here: 70.3 us
  Pallas kernels  69.5 us (99%)
  between operations  0.8 us (1%)
    pallas_call x1, Pallas kernels, body(): pl.pallas_call(kernel, out_shape=shapes, in_specs=[pl.BlockSpec(memory_sp...  67 us
    pallas_call x1, Pallas kernels, body(): pl.pallas_call(hand_over, out_shape=shapes, in_specs=[any_space] * 5, out...  2.49 us

profile of v5, /device:TPU:0, one launch (start us, length us, event | category | flops | bytes accessed | tf_op | source)
XLA Modules:
  0.0 70.3 jit_solution(17660274564867842177)
XLA Ops:
  0.6 67.0 %attention_layer.1 = (bf16[512,512]{1,0:T(8,128)(2,1)}, bf16[512,1024]{1,0:T(8,128)(2,1)}, f32[128,512]{1,0:T(8,128)}, f32[128,128]{1,0:T(8,128)}, f32[128,128]{1,0:T(8,128)}) custom-call(s32[32]{0:T(128)} %doc_ref.1, bf16[512,4096]{1,0:T(8,128)(2,1)} %x_hbm.1, bf16[4096,512]{1,0:T(8,128)(2,1)} %wq_hbm.1, bf16[4096,128]{1,0:T(8,128)(2,1)} %wk_hbm.1, ...), custom_call_target="tpu_custom_call" | custom-call | flops 20000000000 | bytes 13000000 | tf_op jit(solution)/shard_map/attention_layer/pallas_call | solution.py:672
  67.7 2.5 %hand_over.1 = (bf16[512,512]{1,0:T(8,128)(2,1)}, bf16[512,1024]{1,0:T(8,128)(2,1)}, f32[128,512]{1,0:T(8,128)}, f32[128,128]{1,0:T(8,128)}, f32[128,128]{1,0:T(8,128)}) custom-call(bf16[512,512]{1,0:T(8,128)(2,1)} %get-tuple-element.10.refs_0_, bf16[512,1024]{1,0:T(8,128)(2,1)} %get-tuple-element.11.refs_1_, f32[128,512]{1,0:T(8,128)} %get-tuple-element.12.refs_2_, ...), custom_call_target="tpu_custom_call" | custom-call | tf_op jit(solution)/shard_map/hand_over/pallas_call | solution.py:717

commit v6 on v5

--- a/solution.py
+++ b/solution.py
@@ -344,14 +344,19 @@
     order = (("x", "y"), ("y", "x")) * 3
     pieces = [(chunk // 2, slice(chunk % 2 * 128, (chunk % 2 + 1) * 128)) for chunk in range(6)]
 
-    def product_half(group, begins):
-        def rows_of(i, carry):
-            part = xT[pl.ds(4 * i, 4), :, begins : begins + TOK].reshape(512, TOK)
-            whole = dot(part, joined[begins : begins + TOK, columns(group)]).reshape(4, 128, 256)
-            pb[group, i] = whole if begins == 0 else pb[group, i] + whole
+    def product_halves(group):
+        def rows_of(j, carry):
+            @pl.when(j == 4)
+            def _():
+                core[group].wait_recv()
+
+            block = j % 4
+            toks = pl.ds(pl.multiple_of((j // 4) * TOK, TOK), TOK)
+            part = xT[pl.ds(4 * block, 4), :, toks].reshape(512, TOK)
+            pb[group, block] += dot(part, joined[toks, columns(group)]).reshape(4, 128, 256)
             return carry
 
-        lax.fori_loop(0, 4, rows_of, 0)
+        lax.fori_loop(0, 8, rows_of, 0)
 
     def product(group):
         def rows_of(i, carry):
@@ -554,6 +559,7 @@
     ring_up(3)
     send_second(0)
     send_second(1)
+    pb[2] = jnp.zeros((4, 4, 128, 256), F32)
 
     @pl.when(has_nxt)
     def _():
@@ -569,9 +575,7 @@
     begin(core[2], *near2)
     ring_down(2)
     ring_down(3)
-    product_half(2, 0)
-    arrive(core[2])
-    product_half(2, TOK)
+    product_halves(2)
     send_first(4)
     send_first(5)
     add(own_term(2))

time: 70.5 us -> 70.6 us (level)
  no operation moved by 1% of the time
where the time goes in v6:
time: 70.6 us; the launch traced here: 70.4 us
  Pallas kernels  69.6 us (99%)
  between operations  0.8 us (1%)
    pallas_call x1, Pallas kernels, body(): pl.pallas_call(kernel, out_shape=shapes, in_specs=[pl.BlockSpec(memory_sp...  67.1 us
    pallas_call x1, Pallas kernels, body(): pl.pallas_call(hand_over, out_shape=shapes, in_specs=[any_space] * 5, out...  2.49 us

profile of v6, /device:TPU:0, one launch (start us, length us, event | category | flops | bytes accessed | tf_op | source)
XLA Modules:
  0.0 70.4 jit_solution(15556041187387155176)
XLA Ops:
  0.6 67.1 %attention_layer.1 = (bf16[512,512]{1,0:T(8,128)(2,1)}, bf16[512,1024]{1,0:T(8,128)(2,1)}, f32[128,512]{1,0:T(8,128)}, f32[128,128]{1,0:T(8,128)}, f32[128,128]{1,0:T(8,128)}) custom-call(s32[32]{0:T(128)} %doc_ref.1, bf16[512,4096]{1,0:T(8,128)(2,1)} %x_hbm.1, bf16[4096,512]{1,0:T(8,128)(2,1)} %wq_hbm.1, bf16[4096,128]{1,0:T(8,128)(2,1)} %wk_hbm.1, ...), custom_call_target="tpu_custom_call" | custom-call | flops 20000000000 | bytes 13000000 | tf_op jit(solution)/shard_map/attention_layer/pallas_call | solution.py:676
  67.8 2.5 %hand_over.1 = (bf16[512,512]{1,0:T(8,128)(2,1)}, bf16[512,1024]{1,0:T(8,128)(2,1)}, f32[128,512]{1,0:T(8,128)}, f32[128,128]{1,0:T(8,128)}, f32[128,128]{1,0:T(8,128)}) custom-call(bf16[512,512]{1,0:T(8,128)(2,1)} %get-tuple-element.10.refs_0_, bf16[512,1024]{1,0:T(8,128)(2,1)} %get-tuple-element.11.refs_1_, f32[128,512]{1,0:T(8,128)} %get-tuple-element.12.refs_2_, ...), custom_call_target="tpu_custom_call" | custom-call | tf_op jit(solution)/shard_map/hand_over/pallas_call | solution.py:721
